TPU v7x, 256 devices: a whole 4x4x8 slice. The times are simulated.
256 devices in a mesh: clus: 64 (over z, x, core), rep: 4 (over y).
Axes of the slice: x: 4, y: 4, z: 8, core: 2. Of those that a mesh axis runs over, the one named last changes fastest.
Arguments:
- density: bfloat16 [1024, 8, 256], P('clus'), may hold values from -6 to 6
- positions: bfloat16 [1024, 3, 256], P('clus'), may hold values from 0 to 1
- areas: bfloat16 [1024, 256], P('clus'), may hold values from 0.29882812 to 3
- near_pairs: int32 [64, 4, 64, 4, 2], P('clus', 'rep'), may hold values from 0 to 1023, as said below
- near_counts: int32 [64, 4, 64], P('clus', 'rep'), may hold values from 1 to 4, as said below
- far_pairs: int32 [64, 4, 64, 2, 2], P('clus', 'rep'), may hold values from 0 to 1023, as said below
- far_counts: int32 [64, 4, 64], P('clus', 'rep'), may hold values from 1 to 2
- far_right: bfloat16 [64, 4, 64, 2, 32, 256], P('clus', 'rep'), may hold values from -0.375 to 0.375
- far_left: bfloat16 [64, 4, 64, 2, 32, 256], P('clus', 'rep'), may hold values from -0.125 to 0.125
Outputs:
- potential: float32 [1024, 8, 256], P('clus')
Inputs may be any that keep to these rules, and one draw needn't show every extreme that they name: `near_pairs`: slot [d, u, e, k] holds a pair (i, j) with i owned by index d of clus and j by index e, where cluster c is owned by index c // 16; i != j; pairs may repeat; slots that are not live hold valid pairs too. `near_counts`: equal to 4 where owner e is within two indices of d along clus, counted around the axis. `far_pairs`: slot [d, u, e, k] holds a pair (i, j) with i owned by index d of clus and j by index e, where cluster c is owned by index c // 16; i != j; its factors stand at the same slot of far_right and far_left; slots that are not live hold valid pairs too.
All inputs are finite; a program needn't handle non-finite values.
Results may differ from a plain program's by a relative error of at most 0.0029.
Values may be sent and summed in bfloat16 or wider, within the bound.
A program may use at most 128 MiB of HBM per device.

v0:
```python
import math

import jax
import jax.numpy as jnp
from jax import lax
from jax.sharding import PartitionSpec as P

softening = 0.01


def build(left_pos, left_area, right_pos, right_area):
    panels = right_pos.shape[-1]
    left_pos = left_pos.astype(jnp.float32)
    right_pos = right_pos.astype(jnp.float32)
    squared = (left_pos[..., 0, :, None] - right_pos[..., 0, None, :]) ** 2
    squared = squared + (left_pos[..., 1, :, None] - right_pos[..., 1, None, :]) ** 2
    squared = squared + (left_pos[..., 2, :, None] - right_pos[..., 2, None, :]) ** 2
    weight_pair = (
        left_area.astype(jnp.float32)[..., :, None] * right_area.astype(jnp.float32)[..., None, :]
    )
    return (weight_pair / (panels * jnp.sqrt(squared + softening))).astype(jnp.bfloat16)


def indicator_matrix(index_ids, cluster_groups):
    return (index_ids[..., None] == jnp.arange(cluster_groups, dtype=jnp.int32)).astype(jnp.float32)


def near_block(pieces):
    pos_row, area_row, dens_row, pos_col, area_col, dens_col = pieces
    tile_set = build(pos_row, area_row, pos_col, area_col)
    row_contributions = jnp.einsum(
        "tab,trb->tra", tile_set, dens_col, preferred_element_type=jnp.float32
    )
    col_terms = jnp.einsum("tab,tra->trb", tile_set, dens_row, preferred_element_type=jnp.float32)
    return (row_contributions, col_terms)


def per_device(
    density, positions, areas, near_pairs, near_counts, far_pairs, far_counts, far_right, far_left
):
    high_precision = lax.Precision.HIGHEST
    cluster_groups, directions, panels = density.shape
    peer_count = lax.axis_size("clus")
    my_index = lax.axis_index("clus")
    near_list = near_pairs[0, 0]
    far_list = far_pairs[0, 0]
    slots_near = near_list.shape[1]
    slots_far = far_list.shape[1]
    live_near = (
        jnp.arange(slots_near, dtype=jnp.int32)[None, :] < near_counts[0, 0][:, None]
    ).astype(jnp.float32)
    live_far = (jnp.arange(slots_far, dtype=jnp.int32)[None, :] < far_counts[0, 0][:, None]).astype(
        jnp.float32
    )
    offsets = (jnp.arange(peer_count, dtype=jnp.int32) * cluster_groups)[:, None]
    needed_rows = jnp.concatenate([near_list[..., 1] - offsets, far_list[..., 1] - offsets], axis=1)
    rows_near = (near_list[..., 0] - my_index * cluster_groups).reshape(-1)
    rows_far = (far_list[..., 0] - my_index * cluster_groups).reshape(-1)
    all_dens, all_pos, all_area = (
        lax.all_gather(density, "clus", axis=0, tiled=True),
        lax.all_gather(positions, "clus", axis=0, tiled=True),
        lax.all_gather(areas, "clus", axis=0, tiled=True),
    )
    global_ids = needed_rows + offsets
    got_dens = all_dens[global_ids]
    got_pos = all_pos[global_ids]
    got_area = all_area[global_ids]
    near_count = peer_count * slots_near
    block_size = math.gcd(near_count, 32)
    block_count = near_count // block_size

    def blocked(values):
        return values.reshape((block_count, block_size) + values.shape[1:])

    col_dens = got_dens[:, :slots_near].reshape(near_count, directions, panels)
    col_pos = got_pos[:, :slots_near].reshape(near_count, 3, panels)
    col_area = got_area[:, :slots_near].reshape(near_count, panels)
    pieces = (
        blocked(positions[rows_near]),
        blocked(areas[rows_near]),
        blocked(density[rows_near]),
        blocked(col_pos),
        blocked(col_area),
        blocked(col_dens),
    )
    near_rows, near_cols = lax.map(near_block, pieces)
    near_rows = near_rows.reshape(near_count, directions, panels) * live_near.reshape(-1, 1, 1)
    near_cols = (
        near_cols.reshape(peer_count, slots_near, directions, panels) * live_near[..., None, None]
    )
    right_f = far_right[0, 0]
    left_f = far_left[0, 0]
    far_dens_col = got_dens[:, slots_near:]
    far_dens_row = density[rows_far].reshape(peer_count, slots_far, directions, panels)
    projected_col = jnp.einsum(
        "pkqs,pkrs->pkqr", right_f, far_dens_col, preferred_element_type=jnp.float32
    ).astype(jnp.bfloat16)
    projected_row = jnp.einsum(
        "pkqs,pkrs->pkqr", left_f, far_dens_row, preferred_element_type=jnp.float32
    ).astype(jnp.bfloat16)
    far_rows = (
        jnp.einsum("pkqr,pkqs->pkrs", projected_col, left_f, preferred_element_type=jnp.float32)
        * live_far[..., None, None]
    )
    far_cols = (
        jnp.einsum("pkqr,pkqs->pkrs", projected_row, right_f, preferred_element_type=jnp.float32)
        * live_far[..., None, None]
    )
    row_share = panels // lax.axis_size("rep")
    row_start = lax.axis_index("rep") * row_share
    self_pos = lax.dynamic_slice_in_dim(positions, row_start, row_share, 2)
    self_area = lax.dynamic_slice_in_dim(areas, row_start, row_share, 1)
    self_tiles = build(self_pos, self_area, positions, areas)
    self_terms = jnp.einsum("cab,crb->cra", self_tiles, density, preferred_element_type=jnp.float32)
    partial_value = lax.dynamic_update_slice_in_dim(
        jnp.zeros((cluster_groups, directions, panels), jnp.float32), self_terms, row_start, 2
    )
    rows_all = jnp.concatenate([rows_near, rows_far])
    terms_all = jnp.concatenate([near_rows, far_rows.reshape(-1, directions, panels)], axis=0)
    partial_value = partial_value + jnp.einsum(
        "tc,trs->crs",
        indicator_matrix(rows_all, cluster_groups),
        terms_all,
        precision=high_precision,
    )
    sent_values = jnp.concatenate([near_cols, far_cols], axis=1)
    reduced_sum = jnp.einsum(
        "ido,idub->ioub",
        indicator_matrix(needed_rows, cluster_groups),
        sent_values,
        precision=high_precision,
    )
    arrived = lax.all_to_all(reduced_sum, "clus", split_axis=0, concat_axis=0, tiled=True)
    partial_value = partial_value + jnp.sum(arrived, axis=0)
    return lax.psum(partial_value, "rep")


def solution(mesh):
    return jax.shard_map(
        per_device,
        mesh=mesh,
        in_specs=(
            P("clus", None, None),
            P("clus", None, None),
            P("clus", None),
            P("clus", "rep", None, None, None),
            P("clus", "rep", None),
            P("clus", "rep", None, None, None),
            P("clus", "rep", None),
            P("clus", "rep", None, None, None, None),
            P("clus", "rep", None, None, None, None),
        ),
        out_specs=P("clus", None, None),
        check_vma=False,
    )
```

profile of v0, /device:TPU:1, one launch (start us, length us, event | category | flops | bytes accessed | tf_op | source)
XLA Modules:
  0.0 630.2 jit_solution(12334333821099820767)
XLA Ops:
  9.0 3.5 gather_fusion.3
  12.5 1.7 gather_fusion.5
  15.5 1.8 gather_fusion.1
  17.3 1.5 gather_fusion.6
  18.9 2.7 fusion.31
  21.6 1.5 copy.66
  23.1 54.8 %all_gather.10 = bf16[1024,256]{1,0:T(8,128)(2,1)S(1)} all-gather(bf16[16,256]{1,0:T(8,128)(2,1)S(1)} %copy-done.2), channel_id=1, replica_groups=mesh['clus'=64,'rep'=4] {'clus'}, dimensions={0}, use_global_device_ids=true | all-gather | bytes 532480 | tf_op jit(solution)/shard_map/all_gather | solution.py:62
  77.9 2.1 gather_fusion.2
  81.5 4.4 all-gather.5.cloned.1.call-done
  85.9 4.1 copy.56
  90.0 3.1 gather_fusion.4
  93.4 73.1 %all-gather.3.cloned.1.call-done = bf16[1024,8,256]{2,1,0:T(8,128)(2,1)} async-done(((bf16[16,8,256]{2,1,0:T(8,128)(2,1)}), bf16[1024,8,256]{2,1,0:T(8,128)(2,1)}) %all-gather.3.cloned.1.call-update) | async-done | bytes 4194320 | tf_op jit(solution)/shard_map/all_gather | solution.py:60
  166.5 4.2 gather_fusion
  170.7 1.3 slice.98
  172.0 201.5 %while.12 = (s32[]{:T(128)}, f32[8,32,8,256]{3,1,0,2:T(8,128)}, f32[8,32,8,256]{3,2,1,0:T(8,128)}, bf16[8,32,8,256]{3,2,1,0:T(8,128)(2,1)S(1)}, bf16[8,32,256]{2...) while((s32[]{:T(128)}, f32[8,32,8,256]{3,1,0,2:T(8,128)}, ...), condition=%wide.region_1.2_spmd, body=%wide.region_0.1_spmd.sunk | while | flops 121700352 | bytes 2622589 | solution.py:86
  172.7 0.8 bitcast_convert_fusion.6
  173.6 12.9 %fusion.69 = f32[1,32,8,256]{3,2,1,0:T(8,128)S(1)} fusion(f32[32,256]{1,0:T(8,128)S(1)} %get-tuple-element.186, f32[32,256]{1,0:T(8,128)S(1)} %get-tuple-element.188, f32[32,256]{1,0:T(8,128)S(1)} %get-tuple-element.189, f32[32,256]{1,0:T(8,128)S(1)} %get-tuple-element.190, f32[32,256]{1,0:T(8,128)S(1)} %get-tuple-element.191, ...), kind=kOutput, calls=%fused_computation.10.clone.1 | convolution fusion | flops 60817408 | bytes 655364 | tf_op jit(solution)/shard_map/while/body/eval_jaxpr/tab,trb->tra/dot_general | solution.py:31
  186.5 9.9 %fusion.70 = f32[8,32,8,256]{3,2,1,0:T(8,128)} fusion(f32[8,32,8,256]{3,2,1,0:T(8,128)} %get-tuple-element.207, s32[]{:T(128)S(6)} %copy.92, f32[32,256]{1,0:T(8,128)S(1)} %get-tuple-element.186, f32[32,256]{1,0:T(8,128)S(1)} %get-tuple-element.188, f32[32,256]{1,0:T(8,128)S(1)} %get-tuple-element.189, f32[32,256]{1,0:T(8,128)S(1)} %get-tuple-element.190, ...), kind=kOutput, calls=%fused_computation.12.clone.1 | convolution fusion | flops 60817408 | bytes 656384 | tf_op jit(solution)/shard_map/while/body/eval_jaxpr/tab,tra->trb/dot_general | solution.py:34
  197.9 0.8 bitcast_convert_fusion.6
  198.8 12.9 %fusion.69 = f32[1,32,8,256]{3,2,1,0:T(8,128)S(1)} fusion(f32[32,256]{1,0:T(8,128)S(1)} %get-tuple-element.186, f32[32,256]{1,0:T(8,128)S(1)} %get-tuple-element.188, f32[32,256]{1,0:T(8,128)S(1)} %get-tuple-element.189, f32[32,256]{1,0:T(8,128)S(1)} %get-tuple-element.190, f32[32,256]{1,0:T(8,128)S(1)} %get-tuple-element.191, ...), kind=kOutput, calls=%fused_computation.10.clone.1 | convolution fusion | flops 60817408 | bytes 655364 | tf_op jit(solution)/shard_map/while/body/eval_jaxpr/tab,trb->tra/dot_general | solution.py:31
  211.6 9.9 %fusion.70 = f32[8,32,8,256]{3,2,1,0:T(8,128)} fusion(f32[8,32,8,256]{3,2,1,0:T(8,128)} %get-tuple-element.207, s32[]{:T(128)S(6)} %copy.92, f32[32,256]{1,0:T(8,128)S(1)} %get-tuple-element.186, f32[32,256]{1,0:T(8,128)S(1)} %get-tuple-element.188, f32[32,256]{1,0:T(8,128)S(1)} %get-tuple-element.189, f32[32,256]{1,0:T(8,128)S(1)} %get-tuple-element.190, ...), kind=kOutput, calls=%fused_computation.12.clone.1 | convolution fusion | flops 60817408 | bytes 656384 | tf_op jit(solution)/shard_map/while/body/eval_jaxpr/tab,tra->trb/dot_general | solution.py:34
  223.1 0.8 bitcast_convert_fusion.6
  223.9 12.9 %fusion.69 = f32[1,32,8,256]{3,2,1,0:T(8,128)S(1)} fusion(f32[32,256]{1,0:T(8,128)S(1)} %get-tuple-element.186, f32[32,256]{1,0:T(8,128)S(1)} %get-tuple-element.188, f32[32,256]{1,0:T(8,128)S(1)} %get-tuple-element.189, f32[32,256]{1,0:T(8,128)S(1)} %get-tuple-element.190, f32[32,256]{1,0:T(8,128)S(1)} %get-tuple-element.191, ...), kind=kOutput, calls=%fused_computation.10.clone.1 | convolution fusion | flops 60817408 | bytes 655364 | tf_op jit(solution)/shard_map/while/body/eval_jaxpr/tab,trb->tra/dot_general | solution.py:31
  236.8 10.0 %fusion.70 = f32[8,32,8,256]{3,2,1,0:T(8,128)} fusion(f32[8,32,8,256]{3,2,1,0:T(8,128)} %get-tuple-element.207, s32[]{:T(128)S(6)} %copy.92, f32[32,256]{1,0:T(8,128)S(1)} %get-tuple-element.186, f32[32,256]{1,0:T(8,128)S(1)} %get-tuple-element.188, f32[32,256]{1,0:T(8,128)S(1)} %get-tuple-element.189, f32[32,256]{1,0:T(8,128)S(1)} %get-tuple-element.190, ...), kind=kOutput, calls=%fused_computation.12.clone.1 | convolution fusion | flops 60817408 | bytes 656384 | tf_op jit(solution)/shard_map/while/body/eval_jaxpr/tab,tra->trb/dot_general | solution.py:34
  248.3 0.8 bitcast_convert_fusion.6
  249.1 12.9 %fusion.69 = f32[1,32,8,256]{3,2,1,0:T(8,128)S(1)} fusion(f32[32,256]{1,0:T(8,128)S(1)} %get-tuple-element.186, f32[32,256]{1,0:T(8,128)S(1)} %get-tuple-element.188, f32[32,256]{1,0:T(8,128)S(1)} %get-tuple-element.189, f32[32,256]{1,0:T(8,128)S(1)} %get-tuple-element.190, f32[32,256]{1,0:T(8,128)S(1)} %get-tuple-element.191, ...), kind=kOutput, calls=%fused_computation.10.clone.1 | convolution fusion | flops 60817408 | bytes 655364 | tf_op jit(solution)/shard_map/while/body/eval_jaxpr/tab,trb->tra/dot_general | solution.py:31
  262.0 9.9 %fusion.70 = f32[8,32,8,256]{3,2,1,0:T(8,128)} fusion(f32[8,32,8,256]{3,2,1,0:T(8,128)} %get-tuple-element.207, s32[]{:T(128)S(6)} %copy.92, f32[32,256]{1,0:T(8,128)S(1)} %get-tuple-element.186, f32[32,256]{1,0:T(8,128)S(1)} %get-tuple-element.188, f32[32,256]{1,0:T(8,128)S(1)} %get-tuple-element.189, f32[32,256]{1,0:T(8,128)S(1)} %get-tuple-element.190, ...), kind=kOutput, calls=%fused_computation.12.clone.1 | convolution fusion | flops 60817408 | bytes 656384 | tf_op jit(solution)/shard_map/while/body/eval_jaxpr/tab,tra->trb/dot_general | solution.py:34
  273.5 0.8 bitcast_convert_fusion.6
  274.3 12.9 %fusion.69 = f32[1,32,8,256]{3,2,1,0:T(8,128)S(1)} fusion(f32[32,256]{1,0:T(8,128)S(1)} %get-tuple-element.186, f32[32,256]{1,0:T(8,128)S(1)} %get-tuple-element.188, f32[32,256]{1,0:T(8,128)S(1)} %get-tuple-element.189, f32[32,256]{1,0:T(8,128)S(1)} %get-tuple-element.190, f32[32,256]{1,0:T(8,128)S(1)} %get-tuple-element.191, ...), kind=kOutput, calls=%fused_computation.10.clone.1 | convolution fusion | flops 60817408 | bytes 655364 | tf_op jit(solution)/shard_map/while/body/eval_jaxpr/tab,trb->tra/dot_general | solution.py:31
  287.2 9.9 %fusion.70 = f32[8,32,8,256]{3,2,1,0:T(8,128)} fusion(f32[8,32,8,256]{3,2,1,0:T(8,128)} %get-tuple-element.207, s32[]{:T(128)S(6)} %copy.92, f32[32,256]{1,0:T(8,128)S(1)} %get-tuple-element.186, f32[32,256]{1,0:T(8,128)S(1)} %get-tuple-element.188, f32[32,256]{1,0:T(8,128)S(1)} %get-tuple-element.189, f32[32,256]{1,0:T(8,128)S(1)} %get-tuple-element.190, ...), kind=kOutput, calls=%fused_computation.12.clone.1 | convolution fusion | flops 60817408 | bytes 656384 | tf_op jit(solution)/shard_map/while/body/eval_jaxpr/tab,tra->trb/dot_general | solution.py:34
  298.7 0.8 bitcast_convert_fusion.6
  299.5 12.9 %fusion.69 = f32[1,32,8,256]{3,2,1,0:T(8,128)S(1)} fusion(f32[32,256]{1,0:T(8,128)S(1)} %get-tuple-element.186, f32[32,256]{1,0:T(8,128)S(1)} %get-tuple-element.188, f32[32,256]{1,0:T(8,128)S(1)} %get-tuple-element.189, f32[32,256]{1,0:T(8,128)S(1)} %get-tuple-element.190, f32[32,256]{1,0:T(8,128)S(1)} %get-tuple-element.191, ...), kind=kOutput, calls=%fused_computation.10.clone.1 | convolution fusion | flops 60817408 | bytes 655364 | tf_op jit(solution)/shard_map/while/body/eval_jaxpr/tab,trb->tra/dot_general | solution.py:31
  312.4 9.9 %fusion.70 = f32[8,32,8,256]{3,2,1,0:T(8,128)} fusion(f32[8,32,8,256]{3,2,1,0:T(8,128)} %get-tuple-element.207, s32[]{:T(128)S(6)} %copy.92, f32[32,256]{1,0:T(8,128)S(1)} %get-tuple-element.186, f32[32,256]{1,0:T(8,128)S(1)} %get-tuple-element.188, f32[32,256]{1,0:T(8,128)S(1)} %get-tuple-element.189, f32[32,256]{1,0:T(8,128)S(1)} %get-tuple-element.190, ...), kind=kOutput, calls=%fused_computation.12.clone.1 | convolution fusion | flops 60817408 | bytes 656384 | tf_op jit(solution)/shard_map/while/body/eval_jaxpr/tab,tra->trb/dot_general | solution.py:34
  323.9 0.8 bitcast_convert_fusion.6
  324.7 12.9 %fusion.69 = f32[1,32,8,256]{3,2,1,0:T(8,128)S(1)} fusion(f32[32,256]{1,0:T(8,128)S(1)} %get-tuple-element.186, f32[32,256]{1,0:T(8,128)S(1)} %get-tuple-element.188, f32[32,256]{1,0:T(8,128)S(1)} %get-tuple-element.189, f32[32,256]{1,0:T(8,128)S(1)} %get-tuple-element.190, f32[32,256]{1,0:T(8,128)S(1)} %get-tuple-element.191, ...), kind=kOutput, calls=%fused_computation.10.clone.1 | convolution fusion | flops 60817408 | bytes 655364 | tf_op jit(solution)/shard_map/while/body/eval_jaxpr/tab,trb->tra/dot_general | solution.py:31
  337.6 9.9 %fusion.70 = f32[8,32,8,256]{3,2,1,0:T(8,128)} fusion(f32[8,32,8,256]{3,2,1,0:T(8,128)} %get-tuple-element.207, s32[]{:T(128)S(6)} %copy.92, f32[32,256]{1,0:T(8,128)S(1)} %get-tuple-element.186, f32[32,256]{1,0:T(8,128)S(1)} %get-tuple-element.188, f32[32,256]{1,0:T(8,128)S(1)} %get-tuple-element.189, f32[32,256]{1,0:T(8,128)S(1)} %get-tuple-element.190, ...), kind=kOutput, calls=%fused_computation.12.clone.1 | convolution fusion | flops 60817408 | bytes 656384 | tf_op jit(solution)/shard_map/while/body/eval_jaxpr/tab,tra->trb/dot_general | solution.py:34
  349.0 0.8 bitcast_convert_fusion.6
  349.9 12.9 %fusion.69 = f32[1,32,8,256]{3,2,1,0:T(8,128)S(1)} fusion(f32[32,256]{1,0:T(8,128)S(1)} %get-tuple-element.186, f32[32,256]{1,0:T(8,128)S(1)} %get-tuple-element.188, f32[32,256]{1,0:T(8,128)S(1)} %get-tuple-element.189, f32[32,256]{1,0:T(8,128)S(1)} %get-tuple-element.190, f32[32,256]{1,0:T(8,128)S(1)} %get-tuple-element.191, ...), kind=kOutput, calls=%fused_computation.10.clone.1 | convolution fusion | flops 60817408 | bytes 655364 | tf_op jit(solution)/shard_map/while/body/eval_jaxpr/tab,trb->tra/dot_general | solution.py:31
  362.7 9.9 %fusion.70 = f32[8,32,8,256]{3,2,1,0:T(8,128)} fusion(f32[8,32,8,256]{3,2,1,0:T(8,128)} %get-tuple-element.207, s32[]{:T(128)S(6)} %copy.92, f32[32,256]{1,0:T(8,128)S(1)} %get-tuple-element.186, f32[32,256]{1,0:T(8,128)S(1)} %get-tuple-element.188, f32[32,256]{1,0:T(8,128)S(1)} %get-tuple-element.189, f32[32,256]{1,0:T(8,128)S(1)} %get-tuple-element.190, ...), kind=kOutput, calls=%fused_computation.12.clone.1 | convolution fusion | flops 60817408 | bytes 656384 | tf_op jit(solution)/shard_map/while/body/eval_jaxpr/tab,tra->trb/dot_general | solution.py:34
  373.5 2.5 copy_multiply_fusion
  376.0 7.1 %fusion.15 = f32[64,16,8,256]{3,1,2,0:T(8,128)} fusion(f32[64,2,8,256]{3,1,2,0:T(2,128)S(1)} %copy-done.8, f32[64,4,8,256]{3,1,2,0:T(4,128)S(1)} %copy_multiply_fusion, s32[64,6]{1,0:T(8,128)S(1)} %copy-done.17), kind=kOutput, calls=%fused_computation.34 | convolution fusion | flops 151787520 | bytes 11535872 | tf_op jit(solution)/shard_map/ido,idub->ioub/dot_general | solution.py:127
  383.2 6.6 %all-to-all-start = ((f32[64,16,8,256]{3,1,2,0:T(8,128)}), f32[64,16,8,256]{3,1,2,0:T(8,128)}, u32[]{:S(2)}, u32[]{:S(2)}) async-start(f32[64,16,8,256]{3,1,2,0:T(8,128)} %fusion.15), calls=%async_computation | async-start | bytes 16777216 | tf_op jit(solution)/shard_map/all_to_all | solution.py:133
  390.5 1.7 fusion.45
  394.2 1.1 fusion.19
  395.8 176.4 %all-to-all-done = f32[64,16,8,256]{3,1,2,0:T(8,128)} async-done(((f32[64,16,8,256]{3,1,2,0:T(8,128)}), f32[64,16,8,256]{3,1,2,0:T(8,128)}, u32[]{:S(2)}, u32[]{:S(2)}) %all-to-all-start) | async-done | bytes 8388640 | tf_op jit(solution)/shard_map/all_to_all | solution.py:133
  572.2 4.1 reduce_sum.9
  576.9 45.1 %all-reduce.2.cloned.1.call-done = f32[16,8,256]{2,0,1:T(8,128)} async-done(((f32[16,8,256]{2,0,1:T(8,128)}), f32[16,8,256]{2,0,1:T(8,128)}) %all-reduce.2.cloned.1.call-update) | async-done | bytes 131088 | tf_op jit(solution)/shard_map/psum | solution.py:135
  622.0 1.6 copy.67
  (127 shorter events, 21.5 us)
Async XLA Ops:
  6.5 12.3 %copy-start = (bf16[1,1,64,2,32,256]{5,4,3,2,1,0:T(8,128)(2,1)S(1)}, bf16[1,1,64,2,32,256]{5,4,3,2,1,0:T(8,128)(2,1)}, u32[]{:S(2)}) copy-start(bf16[1,1,64,2,32,256]{5,4,3,2,1,0:T(8,128)(2,1)} %param.19) | copy-start | bytes 6291460
  6.5 6.0 copy-start.4
  6.5 7.7 %copy-start.18 = (s32[1,1,64,2,2]{2,4,3,1,0:T(2,128)S(1)}, s32[1,1,64,2,2]{2,4,3,1,0:T(2,128)}, u32[]{:S(2)}) copy-start(s32[1,1,64,2,2]{2,4,3,1,0:T(2,128)} %param.16) | copy-start | bytes 3076
  6.5 9.0 %copy-start.2 = (bf16[16,256]{1,0:T(8,128)(2,1)S(1)}, bf16[16,256]{1,0:T(8,128)(2,1)}, u32[]{:S(2)}) copy-start(bf16[16,256]{1,0:T(8,128)(2,1)} %param.13) | copy-start | bytes 24580
  6.5 79.3 %all-gather.5.cloned.1.call-start = ((), (), s32[]{:S(2)}) async-start(), calls=%async_computation.2 | async-start | bytes 1597440 | tf_op jit(solution)/shard_map/all_gather | solution.py:61
  7.3 159.2 %all-gather.3.cloned.1.call-start = ((), (), s32[]{:S(2)}) async-start(), calls=%async_computation.1 | async-start | bytes 4259840 | tf_op jit(solution)/shard_map/all_gather | solution.py:60
  8.8 10.0 %copy-start.13 = (s32[64,4,1]{1,0,2:T(8,128)}, s32[64,4,1]{1,0,2:T(8,128)S(1)}, u32[]{:S(2)}) copy-start(s32[64,4,1]{1,0,2:T(8,128)S(1)} %copy.51) | copy-start | bytes 3076
  9.0 9.8 %copy-start.19 = (s32[1,1,64]{2,1,0:T(1,128)S(1)}, s32[1,1,64]{2,1,0:T(1,128)}, u32[]{:S(2)}) copy-start(s32[1,1,64]{2,1,0:T(1,128)} %param.17) | copy-start | bytes 772
  15.4 3.5 copy-start.15
  18.9 59.1 %copy-start.10 = (f32[64,2]{1,0:T(8,128)}, f32[64,2]{1,0:T(8,128)S(1)}, u32[]{:S(2)}) copy-start(f32[64,2]{1,0:T(8,128)S(1)} %fusion.50) | copy-start | bytes 1540
  21.6 59.2 %copy-start.20 = (s32[1,1,64]{2,1,0:T(1,128)S(1)}, s32[1,1,64]{2,1,0:T(1,128)}, u32[]{:S(2)}) copy-start(s32[1,1,64]{2,1,0:T(1,128)} %param.15) | copy-start | bytes 772
  373.5 2.5 copy-start.8
  373.5 2.6 copy-start.17
  383.2 6.7 %copy-start.3 = (bf16[16,256]{1,0:T(8,128)(2,1)S(1)}, bf16[16,256]{1,0:T(8,128)(2,1)}, u32[]{:S(2)}) copy-start(bf16[16,256]{1,0:T(8,128)(2,1)} %param.13) | copy-start | bytes 24580
  383.2 6.7 %copy-start.14 = (s32[64,4,1]{1,0,2:T(8,128)S(1)}, s32[64,4,1]{1,0,2:T(8,128)}, u32[]{:S(2)}) copy-start(s32[64,4,1]{1,0,2:T(8,128)} %copy-done.13) | copy-start | bytes 3076
  383.2 6.8 %copy-start.16 = (s32[64,2,1]{1,0,2:T(8,128)S(1)}, s32[64,2,1]{1,0,2:T(8,128)}, u32[]{:S(2)}) copy-start(s32[64,2,1]{1,0,2:T(8,128)} %copy-done.15) | copy-start | bytes 1540
  383.2 6.9 %copy-start.12 = (f32[64,4]{1,0:T(8,128)S(1)}, f32[64,4]{1,0:T(8,128)}, u32[]{:S(2)}) copy-start(f32[64,4]{1,0:T(8,128)} %fusion.49) | copy-start | bytes 3076
  383.2 7.1 %copy-start.1 = (bf16[16,3,256]{2,0,1:T(8,128)(2,1)S(1)}, bf16[16,3,256]{2,0,1:T(8,128)(2,1)}, u32[]{:S(2)}) copy-start(bf16[16,3,256]{2,0,1:T(8,128)(2,1)} %param.12) | copy-start | bytes 73732
  383.2 7.3 %copy-start.5 = (bf16[16,8,256]{2,1,0:T(8,128)(2,1)S(1)}, bf16[16,8,256]{2,1,0:T(8,128)(2,1)}, u32[]{:S(2)}) copy-start(bf16[16,8,256]{2,1,0:T(8,128)(2,1)} %param.11) | copy-start | bytes 196612
  383.2 189.0 %all-to-all-start = ((f32[64,16,8,256]{3,1,2,0:T(8,128)}), f32[64,16,8,256]{3,1,2,0:T(8,128)}, u32[]{:S(2)}, u32[]{:S(2)}) async-start(f32[64,16,8,256]{3,1,2,0:T(8,128)} %fusion.15), calls=%async_computation | async-start | bytes 16777216 | tf_op jit(solution)/shard_map/all_to_all | solution.py:133
  389.8 232.2 %all-reduce.2.cloned.1.call-start = ((), (), s32[]{:S(2)}) async-start(), calls=%async_computation.3 | async-start | bytes 262144 | tf_op jit(solution)/shard_map/psum | solution.py:135
  390.3 1.9 copy-start.6
  390.3 2.1 copy-start.7
  390.5 2.5 copy-start.11
  392.3 1.6 copy-start.9
Sparse Core Ops, SparseCore 0:
  10.0 75.8 all-gather.4
  88.6 77.8 all-gather.2
  577.1 44.8 all-reduce.1
where the time goes:
time: 634 us; the launch traced here: 630 us
  waiting for transfers between devices  300 us (47%)
  matrix products  196 us (31%)
  blocking collectives  54.8 us (9%)
  local copies, waits for them, and re-layouts  37.5 us (6%)
  other arithmetic  21 us (3%)
  between operations  13.5 us (2%)
  starting transfers between devices  6.68 us (1%)
    all_to_all x1, waiting for transfers between devices, per_device(): lax.all_to_all(reduced_sum, 'clus', split_axis=0, concat_axis=0, tiled=True)  176 us
    dot_general x8, matrix products, near_block(): jnp.einsum('tab,trb->tra', tile_set, dens_col, preferred_element_type=jnp...  103 us
    dot_general x8, matrix products, near_block(): jnp.einsum('tab,tra->trb', tile_set, dens_row, preferred_element_type=jnp...  79.5 us
    all_gather x1, waiting for transfers between devices, per_device(): lax.all_gather(density, 'clus', axis=0, tiled=True)  73.1 us
    all_gather x1, blocking collectives, per_device(): lax.all_gather(areas, 'clus', axis=0, tiled=True)  54.8 us
    psum x1, waiting for transfers between devices, per_device(): return lax.psum(partial_value, 'rep')  45.1 us
  transfers between devices with their start and end apart: 4, of which 4 were waited for; matrix products, arithmetic and copies ran while one was open for 5% of the time, Pallas kernels for 0%

commit v1 on v0

v1 whole, which is shorter than its diff:
```python
import functools

import jax
import jax.numpy as jnp
from jax import lax
from jax.experimental import pallas as pl
from jax.experimental.pallas import tpu as pltpu
from jax.sharding import Mesh, PartitionSpec as P

f32=jnp.float32; bf16=jnp.bfloat16
NA=128; NB=32; NSELF=4; NBT=37
KF=48
G=16

def split3(v):
    h = v.astype(bf16).astype(f32)
    m = (v-h).astype(bf16).astype(f32)
    l = (v-h-m).astype(bf16).astype(f32)
    return h,m,l

def feats(pack_ref, b, vref, left):
    X=[pack_ref[b,128+16*k:144+16*k,:].astype(f32)-0.5 for k in range(3)]
    a=pack_ref[b,176:192,:].astype(f32)
    w=256.0/(a*a)
    n=(X[0]*X[0]+X[1]*X[1]+X[2]*X[2]+0.005)*w
    s=-2.0 if left else 1.0
    rows=[n,w] if left else [w,n]
    rows+= [X[k]*(s*w) for k in range(3)]
    for k,r in enumerate(rows):
        vref[0,pl.ds(k,16,stride=8),:]=r[:,:128]
        vref[1,pl.ds(k,16,stride=8),:]=r[:,128:]

def row8(vref,o):
    return jnp.concatenate([vref[0,pl.ds(o,8),:],vref[1,pl.ds(o,8),:]],1)

def near_kernel(info, pa_ref, pb_ref, own_ref, acca_ref, accb_ref, vl, lf, rt, da, db, sa, sb, ub, ii, jj):
    own = lax.axis_index("x")*2+lax.axis_index("c")
    y = lax.axis_index("y")
    vl[...]=jnp.zeros_like(vl)
    def prep_a(b,_):
        feats(pa_ref,b,vl,True)
        for c in range(16):
            h,m,l=split3(row8(vl,8*c))
            lf[b*16+c]=jnp.concatenate([h,h,m,m,h,l],0).astype(bf16)
        for c in range(0,16,2):
            d=pa_ref[b,8*c:8*c+16,:].astype(f32)
            da[b*16+c]=d[:8]; da[b*16+c+1]=d[8:]
        return 0
    lax.fori_loop(0,8,prep_a,0)
    def right(v):
        h,m,l=split3(v)
        return jnp.concatenate([h,m,h,m,l,h],0).T.astype(bf16)
    def prep_b(b,_):
        feats(pb_ref,b,vl,False)
        for c in range(16):
            rt[b*16+c]=right(row8(vl,8*c))
        for c in range(0,16,2):
            d=pb_ref[b,8*c:8*c+16,:].astype(f32)
            db[b*16+c]=d[:8]; db[b*16+c+1]=d[8:]
        return 0
    lax.fori_loop(0,2,prep_b,0)
    feats(own_ref,0,vl,False)
    for s in range(NSELF):
        c=4*y+s
        rt[32+s]=right(row8(vl,pl.multiple_of(8*c,8)))
        db[32+s]=da[own*16+c]
        ii[s]=own*16+c
        jj[s]=32+s
    rt[36]=rt[0]
    db[36]=jnp.zeros((8,256),f32)
    sa[...]=jnp.zeros_like(sa); sb[...]=jnp.zeros_like(sb)
    def comp(src,pos):
        base=(src//4)*16
        for zh in range(2):
            for k in range(4):
                ii[pos+k]=base+info[src,zh*4+k]
                jj[pos+k]=zh*16+info[src,8+zh*4+k]
            pos=pos+info[src,16+zh]
        return pos
    n=lax.fori_loop(0,32,comp,NSELF)
    for k in range(G):
        ii[n+k]=0; jj[n+k]=36
    steps=(n+G-1)//G
    def build(t,slot):
        for g in range(G):
            i=ii[t*G+g]; j=jj[t*G+g]
            d2=jnp.dot(rt[j],lf[i],preferred_element_type=f32)
            ub[slot,g]=lax.rsqrt(d2).astype(bf16)
    def apply(t,slot):
        for g in range(G):
            i=ii[t*G+g]; j=jj[t*G+g]
            u=ub[slot,g]
            r=jnp.dot(db[j].astype(bf16),u,preferred_element_type=f32)
            c=lax.dot_general(da[i].astype(bf16),u,(((1,),(1,)),((),())),preferred_element_type=f32)
            sa[i]=sa[i]+r
            sb[j]=sb[j]+c
    build(0,0)
    def step(t,_):
        slot=lax.rem(t,2)
        apply(t-1,1-slot)
        build(t,slot)
        return 0
    lax.fori_loop(1,steps,step,0)
    apply(steps-1,lax.rem(steps-1,2))
    def out_a(b,_):
        for c in range(0,16,2):
            acca_ref[b,8*c:8*c+16,:]=jnp.concatenate([sa[b*16+c],sa[b*16+c+1]],0).astype(bf16)
        return 0
    lax.fori_loop(0,8,out_a,0)
    accb_ref[...]=sb[0:32]

def near_call(info,pa,pb,own):
    V=pl.BlockSpec(memory_space=pltpu.VMEM)
    return pl.pallas_call(near_kernel,
        out_shape=(jax.ShapeDtypeStruct((8,128,256),bf16),jax.ShapeDtypeStruct((32,8,256),f32)),
        in_specs=[pl.BlockSpec(memory_space=pltpu.SMEM),V,V,V],out_specs=(V,V),
        scratch_shapes=[pltpu.VMEM((2,128,128),f32),pltpu.VMEM((NA,KF,256),bf16),pltpu.VMEM((NBT,256,KF),bf16),
            pltpu.VMEM((NA,8,256),f32),pltpu.VMEM((NBT,8,256),f32),pltpu.VMEM((NA,8,256),f32),pltpu.VMEM((NBT,8,256),f32),
            pltpu.VMEM((2,G,256,256),bf16),pltpu.SMEM((280,),jnp.int32),pltpu.SMEM((280,),jnp.int32)],
        compiler_params=pltpu.CompilerParams(vmem_limit_bytes=48*1024*1024),
    )(info,pa,pb,own)


MESH = pl.DeviceIdType.MESH
VM = pl.BlockSpec(memory_space=pltpu.VMEM)
SM = pl.BlockSpec(memory_space=pltpu.SMEM)


def coords():
    return tuple(lax.axis_index(n) for n in ("z", "x", "c", "y"))


def plane_peer(flat):
    return flat // 8, lax.rem(flat // 4, 2), lax.rem(flat, 4)


def gather_kernel(pack, info, pa, pb, got, ssem, rsem, isend, irecv, lsem):
    z, x, c, y = coords()
    me = (x * 2 + c) * 4 + y
    row = x * 2 + c
    barrier = pltpu.get_barrier_semaphore()

    def greet(t, _):
        px, pc, py = plane_peer(lax.rem(me + t, 32))
        pl.semaphore_signal(barrier, inc=1, device_id=(z, px, pc, py), device_id_type=MESH)
        return 0

    lax.fori_loop(1, 32, greet, 0)

    def greet_z(t, _):
        pl.semaphore_signal(barrier, inc=1, device_id=(lax.rem(z + t, 8), x, c, y), device_id_type=MESH)
        return 0

    lax.fori_loop(1, 8, greet_z, 0)
    own_a = pltpu.make_async_copy(pack, pa.at[row], lsem.at[0])
    own_a.start()
    own_i = pltpu.make_async_copy(info.at[me], got.at[me], lsem.at[1])
    own_i.start()
    owner = lax.rem(z, 4) == y
    half = z // 4

    @pl.when(owner)
    def _():
        cp = pltpu.make_async_copy(pack, pb.at[half], lsem.at[2])
        cp.start()
        cp.wait()

    pl.semaphore_wait(barrier, 38)

    def copy_b(t, h):
        return pltpu.make_async_remote_copy(
            src_ref=pack, dst_ref=pb.at[h], send_sem=ssem.at[8 + t], recv_sem=rsem.at[8 + h],
            device_id=(lax.rem(z + t, 8), x, c, y), device_id_type=MESH)

    @pl.when(owner)
    def _():
        def send(t, _):
            copy_b(t, half).start()
            return 0
        lax.fori_loop(1, 8, send, 0)

    def copy_a(t, slot):
        p = lax.rem(row + t, 8)
        return pltpu.make_async_remote_copy(
            src_ref=pack, dst_ref=pa.at[slot], send_sem=ssem.at[t], recv_sem=rsem.at[slot],
            device_id=(z, p // 2, lax.rem(p, 2), y), device_id_type=MESH)

    def send_a(t, _):
        copy_a(t, row).start()
        return 0

    lax.fori_loop(1, 8, send_a, 0)

    def copy_i(t, slot):
        p = lax.rem(me + t, 32)
        px, pc, py = plane_peer(p)
        return pltpu.make_async_remote_copy(
            src_ref=info.at[p], dst_ref=got.at[slot], send_sem=isend.at[t], recv_sem=irecv.at[slot],
            device_id=(z, px, pc, py), device_id_type=MESH)

    def send_i(t, _):
        copy_i(t, me).start()
        return 0

    lax.fori_loop(1, 32, send_i, 0)
    own_a.wait()
    own_i.wait()

    def wait_a(t, _):
        cp = copy_a(t, lax.rem(row + t, 8))
        cp.wait_send()
        cp.wait_recv()
        return 0

    lax.fori_loop(1, 8, wait_a, 0)

    def wait_i(t, _):
        cp = copy_i(t, lax.rem(me + t, 32))
        cp.wait_send()
        cp.wait_recv()
        return 0

    lax.fori_loop(1, 32, wait_i, 0)
    for h in range(2):
        @pl.when(jnp.logical_not(owner & (half == h)))
        def _(h=h):
            copy_b(1, h).wait_recv()

    @pl.when(owner)
    def _():
        def done(t, _):
            copy_b(t, half).wait_send()
            return 0
        lax.fori_loop(1, 8, done, 0)


def gather_call(pack, info):
    return pl.pallas_call(
        gather_kernel,
        out_shape=(jax.ShapeDtypeStruct((8, 192, 256), bf16), jax.ShapeDtypeStruct((2, 192, 256), bf16),
                   jax.ShapeDtypeStruct((32, 1, 128), jnp.int32)),
        in_specs=[VM, VM], out_specs=(VM, VM, VM),
        scratch_shapes=[pltpu.SemaphoreType.DMA((16,)), pltpu.SemaphoreType.DMA((10,)),
                        pltpu.SemaphoreType.DMA((32,)), pltpu.SemaphoreType.DMA((32,)),
                        pltpu.SemaphoreType.DMA((3,))],
        compiler_params=pltpu.CompilerParams(collective_id=1, has_side_effects=True),
    )(pack, info)


def reduce_kernel(acca, accb, far, out, ra, rb, total, ry, part, ssem, rsem, lsem):
    z, x, c, y = coords()
    row = x * 2 + c
    owner = lax.rem(z, 4) == y
    half = z // 4
    barrier = pltpu.get_barrier_semaphore()

    def peer_row(t):
        p = lax.rem(row + t, 8)
        return (z, p // 2, lax.rem(p, 2), y)

    def peer_y(t):
        return (z, x, c, lax.rem(y + t, 4))

    def greet(t, _):
        pl.semaphore_signal(barrier, inc=1, device_id=peer_row(t), device_id_type=MESH)
        return 0

    lax.fori_loop(1, 8, greet, 0)

    def greet_z(t, _):
        pl.semaphore_signal(barrier, inc=1, device_id=(lax.rem(z + t, 8), x, c, y), device_id_type=MESH)
        return 0

    lax.fori_loop(1, 8, greet_z, 0)

    def greet_y(t, _):
        pl.semaphore_signal(barrier, inc=1, device_id=peer_y(t), device_id_type=MESH)
        return 0

    lax.fori_loop(1, 4, greet_y, 0)
    pl.semaphore_wait(barrier, 17)

    def copy_a(t, slot):
        p = lax.rem(row + t, 8)
        return pltpu.make_async_remote_copy(
            src_ref=acca.at[p], dst_ref=ra.at[slot], send_sem=ssem.at[t], recv_sem=rsem.at[slot],
            device_id=peer_row(t), device_id_type=MESH)

    def copy_b(h, slot):
        return pltpu.make_async_remote_copy(
            src_ref=accb.at[h], dst_ref=rb.at[slot], send_sem=ssem.at[8 + h], recv_sem=rsem.at[8 + slot],
            device_id=(h * 4 + y, x, c, y), device_id_type=MESH)

    for h in range(2):
        @pl.when(jnp.logical_not(owner & (half == h)))
        def _(h=h):
            copy_b(h, z).start()

    def send_a(t, _):
        copy_a(t, row).start()
        return 0

    lax.fori_loop(1, 8, send_a, 0)
    total[...] = far[...] + acca[row].astype(f32)

    @pl.when(owner)
    def _():
        total[...] += accb[half].astype(f32)

    def recv_a(t, _):
        s = lax.rem(row + 8 - t, 8)
        copy_a(t, s).wait_recv()
        total[...] += ra[s].astype(f32)
        return 0

    lax.fori_loop(1, 8, recv_a, 0)

    @pl.when(owner)
    def _():
        def recv_b(t, _):
            s = lax.rem(z + t, 8)
            copy_b(0, s).wait_recv()
            total[...] += rb[s].astype(f32)
            return 0
        lax.fori_loop(1, 8, recv_b, 0)

    def copy_y(t, slot):
        q = lax.rem(y + t, 4)
        return pltpu.make_async_remote_copy(
            src_ref=total.at[pl.ds(pl.multiple_of(q * 32, 32), 32)], dst_ref=ry.at[slot],
            send_sem=ssem.at[10 + t], recv_sem=rsem.at[16 + slot],
            device_id=peer_y(t), device_id_type=MESH)

    for t in range(1, 4):
        copy_y(t, y).start()
    part[...] = total[pl.ds(pl.multiple_of(y * 32, 32), 32), :]
    for t in range(1, 4):
        s = lax.rem(y + t, 4)
        copy_y(t, s).wait_recv()
        part[...] += ry[s]

    def copy_o(t, slot):
        return pltpu.make_async_remote_copy(
            src_ref=part, dst_ref=out.at[pl.ds(pl.multiple_of(slot * 32, 32), 32)],
            send_sem=ssem.at[14 + t], recv_sem=rsem.at[20 + slot],
            device_id=peer_y(t), device_id_type=MESH)

    for t in range(1, 4):
        copy_o(t, y).start()
    own = pltpu.make_async_copy(part, out.at[pl.ds(pl.multiple_of(y * 32, 32), 32)], lsem)
    own.start()
    own.wait()

    for t in range(1, 4):
        copy_o(t, lax.rem(y + t, 4)).wait_recv()

    def done_a(t, _):
        copy_a(t, row).wait_send()
        return 0

    lax.fori_loop(1, 8, done_a, 0)
    for h in range(2):
        @pl.when(jnp.logical_not(owner & (half == h)))
        def _(h=h):
            copy_b(h, z).wait_send()
    for t in range(1, 4):
        copy_y(t, y).wait_send()
        copy_o(t, y).wait_send()


def reduce_call(acca, accb, far):
    return pl.pallas_call(
        reduce_kernel,
        out_shape=jax.ShapeDtypeStruct((128, 256), f32),
        in_specs=[VM, VM, VM], out_specs=VM,
        scratch_shapes=[pltpu.VMEM((8, 128, 256), bf16), pltpu.VMEM((8, 128, 256), bf16),
                        pltpu.VMEM((128, 256), f32), pltpu.VMEM((4, 32, 256), f32), pltpu.VMEM((32, 256), f32),
                        pltpu.SemaphoreType.DMA((18,)), pltpu.SemaphoreType.DMA((24,)), pltpu.SemaphoreType.DMA],
        compiler_params=pltpu.CompilerParams(collective_id=2, has_side_effects=True),
    )(acca, accb, far)


def block_mask(parts):
    r = lax.broadcasted_iota(jnp.int32, (64, 256), 0) // 8
    k = lax.broadcasted_iota(jnp.int32, (64, 256), 1) // 32
    return jnp.where(r == k, 1.0, 0.0)


def through(dens, first, second, mask):
    p = lax.dot_general(dens, first, (((1,), (1,)), ((), ())), preferred_element_type=f32)
    p = (p.astype(bf16).astype(f32) * mask).astype(bf16)
    return jnp.dot(p, second, preferred_element_type=f32)


def place(e):
    z = e // 8
    return (lax.rem(e, 8) * 4 + lax.rem(z, 4)) * 2 + z // 4


def far_cols_kernel(pairs, counts, left, right, dens, out, d32):
    for k in range(8):
        v = dens[16 * k:16 * k + 16, :].astype(f32)
        d32[2 * k] = v[:8]
        d32[2 * k + 1] = v[8:]
    mask = block_mask(8)

    def step(b, _):
        rows = pl.ds(pl.multiple_of(b * 256, 256), 256)
        ds = []
        for s in range(8):
            e, k = b * 4 + s // 2, s % 2
            i = lax.rem(pairs[e, 2 * k], 16)
            ds.append(jnp.where(k < counts[e], d32[i], 0.0))
        r = through(jnp.concatenate(ds, 0).astype(bf16), left[rows, :], right[rows, :], mask)
        for s in range(4):
            o = place(b * 4 + s) * 16
            out[pl.ds(pl.multiple_of(o, 16), 16), :] = r[16 * s:16 * s + 16].astype(bf16)
        return 0

    lax.fori_loop(0, 16, step, 0, unroll=2)


def far_cols_call(pairs, counts, left, right, dens):
    return pl.pallas_call(
        far_cols_kernel,
        out_shape=jax.ShapeDtypeStruct((1024, 256), bf16),
        in_specs=[SM, SM, VM, VM, VM], out_specs=VM,
        scratch_shapes=[pltpu.VMEM((16, 8, 256), f32)],
        compiler_params=pltpu.CompilerParams(vmem_limit_bytes=32 * 1024 * 1024),
    )(pairs, counts, left, right, dens)


def pick_kernel(info, pb, out, d32):
    for h in range(2):
        for k in range(8):
            v = pb[h, 16 * k:16 * k + 16, :].astype(f32)
            d32[16 * h + 2 * k] = v[:8]
            d32[16 * h + 2 * k + 1] = v[8:]

    def step(s, _):
        for h in range(2):
            a = info[s, 18 + 2 * h]
            b = info[s, 19 + 2 * h]
            v = jnp.concatenate([d32[h * 16 + a], d32[h * 16 + b]], 0).astype(bf16)
            out[pl.ds(pl.multiple_of(s * 32 + 16 * h, 16), 16), :] = v
        return 0

    lax.fori_loop(0, 32, step, 0, unroll=4)


def pick_call(info, pb):
    return pl.pallas_call(
        pick_kernel,
        out_shape=jax.ShapeDtypeStruct((1024, 256), bf16),
        in_specs=[SM, VM], out_specs=VM,
        scratch_shapes=[pltpu.VMEM((32, 8, 256), f32)],
        compiler_params=pltpu.CompilerParams(vmem_limit_bytes=32 * 1024 * 1024),
    )(info, pb)


def far_rows_kernel(pairs, counts, info, left, right, dens, cols, accb_in, rows_out, cols_out, acc, accb):
    mask = block_mask(8)
    acc[...] = jnp.zeros_like(acc)
    accb[...] = accb_in[...]

    def step(b, _):
        rows = pl.ds(pl.multiple_of(b * 256, 256), 256)
        ds = []
        for s in range(4):
            o = place(b * 4 + s) * 16
            ds.append(dens[pl.ds(pl.multiple_of(o, 16), 16), :])
        r = through(jnp.concatenate(ds, 0), right[rows, :], left[rows, :], mask)
        for s in range(8):
            e, k = b * 4 + s // 2, s % 2
            i = lax.rem(pairs[e, 2 * k], 16)
            acc[i] += jnp.where(k < counts[e], r[8 * s:8 * s + 8], 0.0)
        return 0

    lax.fori_loop(0, 16, step, 0, unroll=2)

    def add(s, _):
        for h in range(2):
            v = cols[pl.ds(pl.multiple_of(s * 32 + 16 * h, 16), 16), :].astype(f32)
            accb[h * 16 + info[s, 18 + 2 * h]] += v[:8]
            accb[h * 16 + info[s, 19 + 2 * h]] += v[8:]
        return 0

    lax.fori_loop(0, 32, add, 0, unroll=4)
    for k in range(16):
        rows_out[8 * k:8 * k + 8, :] = acc[k]
    for h in range(2):
        for k in range(8):
            cols_out[h, 16 * k:16 * k + 16, :] = jnp.concatenate(
                [accb[16 * h + 2 * k], accb[16 * h + 2 * k + 1]], 0).astype(bf16)


def far_rows_call(pairs, counts, info, left, right, dens, cols, accb):
    return pl.pallas_call(
        far_rows_kernel,
        out_shape=(jax.ShapeDtypeStruct((128, 256), f32), jax.ShapeDtypeStruct((2, 128, 256), bf16)),
        in_specs=[SM, SM, SM, VM, VM, VM, VM, VM], out_specs=(VM, VM),
        scratch_shapes=[pltpu.VMEM((16, 8, 256), f32), pltpu.VMEM((32, 8, 256), f32)],
        compiler_params=pltpu.CompilerParams(vmem_limit_bytes=32 * 1024 * 1024),
    )(pairs, counts, info, left, right, dens, cols, accb)


def per_device(density, positions, areas, near_pairs, near_counts, far_pairs, far_counts, far_right, far_left):
    pack = jnp.concatenate(
        [density.reshape(128, 256), positions.transpose(1, 0, 2).reshape(48, 256), areas], axis=0)
    near = near_pairs.reshape(2, 4, 4, 2, 4, 2)
    near = near.transpose(2, 3, 1, 5, 0, 4).reshape(32, 16) % 16
    ncnt = near_counts.reshape(2, 4, 4, 2).transpose(2, 3, 1, 0).reshape(32, 2)
    fcol = far_pairs[..., 1].reshape(2, 4, 4, 2, 2).transpose(2, 3, 1, 0, 4).reshape(32, 4) % 16
    info = jnp.concatenate([near, ncnt, fcol, jnp.zeros((32, 106), jnp.int32)], axis=1).reshape(32, 1, 128)
    pairs = far_pairs.reshape(64, 4)
    counts = far_counts.reshape(64)
    left = far_left.reshape(4096, 256)
    right = far_right.reshape(4096, 256)

    cols = far_cols_call(pairs, counts, left, right, pack[:128])
    cols = lax.all_to_all(cols.reshape(32, 32, 256), ("x", "c", "y"), 0, 0, tiled=True).reshape(1024, 256)
    pa, pb, got = gather_call(pack, info)
    got = got.reshape(32, 128)
    dens = pick_call(got, pb)
    dens = lax.all_to_all(dens.reshape(32, 32, 256), ("x", "c", "y"), 0, 0, tiled=True).reshape(1024, 256)
    acca, accb = near_call(got, pa, pb, pack[None])
    rows, accb = far_rows_call(pairs, counts, got, left, right, dens, cols, accb)
    out = reduce_call(acca, accb, rows)
    return out.reshape(16, 8, 256)


def solution(mesh):
    grid = Mesh(mesh.devices.reshape(8, 4, 2, 4), ("z", "x", "c", "y"))
    d = ("z", "x", "c")
    return jax.shard_map(
        per_device,
        mesh=grid,
        in_specs=(
            P(d, None, None),
            P(d, None, None),
            P(d, None),
            P(d, "y", None, None, None),
            P(d, "y", None),
            P(d, "y", None, None, None),
            P(d, "y", None),
            P(d, "y", None, None, None, None),
            P(d, "y", None, None, None, None),
        ),
        out_specs=P(d, None, None),
        check_vma=False,
    )
```

time: 634 us -> 118 us (0.19)
  waiting for transfers between devices: 300 us -> 1.3 us
  matrix products: 196 us -> 0 us
  Pallas kernels: 0 us -> 84.2 us
  blocking collectives: 54.8 us -> 0 us
  local copies, waits for them, and re-layouts: 37.5 us -> 17.5 us
  other arithmetic: 21 us -> 3.57 us
  between operations: 13.5 us -> 0.17 us
    dot_general x22 -> x0, matrix products: 196 us -> none  [the longest x8 103 us: near_block(): jnp.einsum('tab,trb->tra', tile_set, dens_col, preferred_element_type=jnp...]
    all_to_all x1 -> x2, waiting for transfers between devices: 176 us -> 1.3 us  [the longest x1 1.3 us: per_device(): lax.all_to_all(dens.reshape(32, 32, 256), ('x', 'c', 'y'), 0, 0, tiled=True)]
    pallas_call x0 -> x6, Pallas kernels: none -> 84.2 us  [the longest x1 26 us: gather_call(): pl.pallas_call(gather_kernel, out_shape=(jax.ShapeDtypeStruct((8, 192, 25...]
    all_gather x2 -> x0, waiting for transfers between devices: 77.5 us -> none  [the longest x1 73.1 us: per_device(): lax.all_gather(density, 'clus', axis=0, tiled=True)]
    all_gather x1 -> x0, blocking collectives: 54.8 us -> none  [per_device(): lax.all_gather(areas, 'clus', axis=0, tiled=True)]
    psum x1 -> x0, waiting for transfers between devices: 45.1 us -> none  [per_device(): return lax.psum(partial_value, 'rep')]
    gather x8 -> x0, local copies, waits for them, and re-layouts: 17.9 us -> none  [the longest x1 4.2 us: per_device(): got_dens = all_dens[global_ids]]
    unnamed x44 -> x37, local copies, waits for them, and re-layouts: 1.14 us -> 15 us
  transfers between devices with their start and end apart: 4 -> 2, of which waited for: 4 -> 1; matrix products, arithmetic and copies ran while one was open for 5% -> 1% of each run, Pallas kernels for 0% -> 22%
where the time goes in v1:
time: 118 us; the launch traced here: 117 us
  Pallas kernels  84.2 us (71%)
  local copies, waits for them, and re-layouts  17.5 us (15%)
  starting transfers between devices  10.5 us (9%)
  other arithmetic  3.57 us (3%)
  waiting for transfers between devices  1.3 us (1%)
    pallas_call x1, Pallas kernels, gather_call(): pl.pallas_call(gather_kernel, out_shape=(jax.ShapeDtypeStruct((8, 192, 25...  26 us
    pallas_call x1, Pallas kernels, reduce_call(): pl.pallas_call(reduce_kernel, out_shape=jax.ShapeDtypeStruct((128, 256),...  24.9 us
    pallas_call x1, Pallas kernels, near_call(): pl.pallas_call(near_kernel, out_shape=(jax.ShapeDtypeStruct((8, 128, 256)...  20.2 us
    unnamed x37, local copies, waits for them, and re-layouts  15 us
    all_to_all x1, starting transfers between devices, per_device(): lax.all_to_all(cols.reshape(32, 32, 256), ('x', 'c', 'y'), 0, 0, tiled=True)  6.3 us
    pallas_call x1, Pallas kernels, far_rows_call(): pl.pallas_call(far_rows_kernel, out_shape=(jax.ShapeDtypeStruct((128, 256...  6.07 us
    pallas_call x1, Pallas kernels, far_cols_call(): pl.pallas_call(far_cols_kernel, out_shape=jax.ShapeDtypeStruct((1024, 256...  5.14 us
    all_to_all x1, starting transfers between devices, per_device(): lax.all_to_all(dens.reshape(32, 32, 256), ('x', 'c', 'y'), 0, 0, tiled=True)  4.19 us
  transfers between devices with their start and end apart: 2, of which 1 were waited for; matrix products, arithmetic and copies ran while one was open for 1% of the time, Pallas kernels for 22%

profile of v1, /device:TPU:1, one launch (start us, length us, event | category | flops | bytes accessed | tf_op | source)
XLA Modules:
  0.0 117.2 jit_solution(2523526914186276575)
XLA Ops:
  0.0 0.9 copy.18
  0.9 0.1 copy.31
  1.0 0.1 reshape.72
  1.1 0.7 slice_reduce_fusion
  1.8 0.1 reshape_squeeze.3
  2.0 0.2 copy.24
  2.2 0.1 reshape.60
  2.3 0.1 copy.25
  2.4 0.5 broadcast.24
  2.9 1.3 %reduce.7 = s32[64]{0:T(128)S(1)} reduce(s32[1,1,64]{2,1,0:T(1,128)} %param.13, s32[]{:T(128)} %broadcast.24), dimensions={0,1}, to_apply=%param.13.reduce_sub_computation.3 | reduce | bytes 516 | tf_op args[4]
  4.2 0.1 reshape.58
  4.3 0.2 copy.33
  4.5 0.1 pad.3.clone
  4.6 1.5 %fusion.2 = (bf16[1,192,256]{2,1,0:T(8,128)(2,1)S(1)}, bf16[192,256]{1,0:T(8,128)(2,1)}) fusion(bf16[16,256]{1,0:T(8,128)(2,1)} %param.11, bf16[48,256]{1,0:T(8,128)(2,1)} %bitcast.47, bf16[128,256]{1,0:T(8,128)(2,1)} %bitcast.34), kind=kLoop, calls=%fused_computation.11 | loop fusion | flops 294912 | bytes 294912 | tf_op jit(solution)/shard_map/broadcast_in_dim | solution.py:526
  6.1 0.7 add_add_fusion
  6.8 26.0 %shard_map.91 = (bf16[8,192,256]{2,1,0:T(8,128)(2,1)}, bf16[2,192,256]{2,1,0:T(8,128)(2,1)}, s32[32,1,128]{2,1,0:T(1,128)}) custom-call(bf16[192,256]{1,0:T(8,128)(2,1)} %get-tuple-element.20.pack, s32[32,1,128]{2,1,0:T(1,128)} %bitcast.44), custom_call_target="tpu_custom_call" | custom-call | tf_op jit(solution)/shard_map/pallas_call | solution.py:238
  32.8 0.0 copy-start.5
  32.8 0.9 copy-done.5
  33.7 0.7 copy-done.11
  34.5 1.9 %shard_map.93 = bf16[1024,256]{1,0:T(8,128)(2,1)} custom-call(s32[32,128]{1,0:T(8,128)S(1)} %bitcast.36, bf16[2,192,256]{2,1,0:T(8,128)(2,1)S(1)} %copy-done.5), custom_call_target="tpu_custom_call" | custom-call | tf_op jit(solution)/shard_map/pallas_call | solution.py:452
  36.3 4.2 %all-to-all-start = ((bf16[32,32,256]{2,1,0:T(8,128)(2,1)}), bf16[32,32,256]{2,1,0:T(8,128)(2,1)S(1)}, u32[]{:S(2)}, u32[]{:S(2)}) async-start(bf16[32,32,256]{2,1,0:T(8,128)(2,1)} %bitcast.15), calls=%async_computation | async-start | bytes 1048576 | tf_op jit(solution)/shard_map/all_to_all | solution.py:525
  40.5 0.8 copy.30.pairs
  41.3 0.0 copy-done
  41.3 1.6 %copy-done.1 = bf16[1,1,64,2,32,256]{5,4,3,2,1,0:T(8,128)(2,1)S(1)} copy-done((bf16[1,1,64,2,32,256]{5,4,3,2,1,0:T(8,128)(2,1)S(1)}, bf16[1,1,64,2,32,256]{5,4,3,2,1,0:T(8,128)(2,1)}, u32[]{:S(2)}) %copy-start.1) | copy-done | bytes 2097176
  42.9 0.8 copy-done.8
  43.7 0.7 copy-done.15
  44.4 5.1 %shard_map.94 = bf16[1024,256]{1,0:T(8,128)(2,1)S(1)} custom-call(s32[64,4]{1,0:T(8,128)S(1)} %copy.30.pairs, s32[64]{0:T(128)S(1)} %bitcast.39, bf16[4096,256]{1,0:T(8,128)(2,1)S(1)} %bitcast.27, bf16[4096,256]{1,0:T(8,128)(2,1)S(1)} %bitcast.29, bf16[128,256]{1,0:T(8,128)(2,1)S(1)} %bitcast.35), custom_call_target="tpu_custom_call" | custom-call | tf_op jit(solution)/shard_map/pallas_call | solution.py:424
  49.5 0.0 copy-start.3
  49.5 0.8 copy-done.3
  50.3 1.3 %all-to-all-done = bf16[32,32,256]{2,1,0:T(8,128)(2,1)S(1)} async-done(((bf16[32,32,256]{2,1,0:T(8,128)(2,1)}), bf16[32,32,256]{2,1,0:T(8,128)(2,1)S(1)}, u32[]{:S(2)}, u32[]{:S(2)}) %all-to-all-start) | async-done | bytes 524320 | tf_op jit(solution)/shard_map/all_to_all | solution.py:525
  51.6 6.3 %all-to-all-start.1 = ((bf16[32,32,256]{2,1,0:T(8,128)(2,1)}), bf16[32,32,256]{2,1,0:T(8,128)(2,1)S(1)}, u32[]{:S(2)}, u32[]{:S(2)}) async-start(bf16[32,32,256]{2,1,0:T(8,128)(2,1)} %bitcast.33), calls=%async_computation.1 | async-start | bytes 1048576 | tf_op jit(solution)/shard_map/all_to_all | solution.py:521
  57.9 0.0 copy-done.6
  57.9 0.0 copy-done.12
  58.0 0.0 copy-start.4
  58.0 1.1 copy-done.4
  59.1 20.2 %shard_map.92 = (bf16[8,128,256]{2,1,0:T(8,128)(2,1)S(1)}, f32[32,8,256]{2,1,0:T(8,128)S(1)}) custom-call(s32[32,128]{1,0:T(8,128)S(1)} %bitcast.37, bf16[8,192,256]{2,1,0:T(8,128)(2,1)S(1)} %copy-done.4, bf16[2,192,256]{2,1,0:T(8,128)(2,1)S(1)} %copy-done.6, bf16[1,192,256]{2,1,0:T(8,128)(2,1)S(1)} %get-tuple-element.19.own_ref), custom_call_target="tpu_custom_call" | custom-call | tf_op jit(solution)/shard_map/pallas_call | solution.py:114
  79.3 0.0 copy-start.7
  79.3 0.8 copy-done.7
  80.1 0.7 copy-done.9
  80.8 0.0 all-to-all-done.1
  80.8 0.0 copy-done.16
  80.8 1.6 %copy-done.2 = bf16[1,1,64,2,32,256]{5,4,3,2,1,0:T(8,128)(2,1)S(1)} copy-done((bf16[1,1,64,2,32,256]{5,4,3,2,1,0:T(8,128)(2,1)S(1)}, bf16[1,1,64,2,32,256]{5,4,3,2,1,0:T(8,128)(2,1)}, u32[]{:S(2)}) %copy-start.2) | copy-done | bytes 2097176
  82.4 0.9 copy-done.10
  83.3 6.1 %shard_map.95 = (f32[128,256]{1,0:T(8,128)S(1)}, bf16[2,128,256]{2,1,0:T(8,128)(2,1)S(1)}) custom-call(s32[64,4]{1,0:T(8,128)S(1)} %copy.30.pairs, s32[64]{0:T(128)S(1)} %bitcast.40, s32[32,128]{1,0:T(8,128)S(1)} %bitcast.38, bf16[4096,256]{1,0:T(8,128)(2,1)S(1)} %bitcast.28, bf16[4096,256]{1,0:T(8,128)(2,1)S(1)} %bitcast.30, ...), custom_call_target="tpu_custom_call" | custom-call | tf_op jit(solution)/shard_map/pallas_call | solution.py:498
  89.4 0.6 copy-done.13
  90.1 0.7 copy-done.14
  90.7 24.9 %shard_map.96 = f32[128,256]{1,0:T(8,128)} custom-call(bf16[8,128,256]{2,1,0:T(8,128)(2,1)} %copy-done.7, bf16[2,128,256]{2,1,0:T(8,128)(2,1)} %copy-done.14, f32[128,256]{1,0:T(8,128)} %copy-done.13), custom_call_target="tpu_custom_call" | custom-call | tf_op jit(solution)/shard_map/pallas_call | solution.py:372
  115.6 1.6 %copy.36 = f32[16,8,256]{2,1,0:T(8,128)} copy(f32[16,8,256]{2,1,0:T(8,128)} %bitcast.41) | data formatting | bytes 262144
  (16 shorter events, 0.0 us)
Async XLA Ops:
  0.0 41.3 %copy-start = (bf16[1,1,64,2,32,256]{5,4,3,2,1,0:T(8,128)(2,1)S(1)}, bf16[1,1,64,2,32,256]{5,4,3,2,1,0:T(8,128)(2,1)}, u32[]{:S(2)}) copy-start(bf16[1,1,64,2,32,256]{5,4,3,2,1,0:T(8,128)(2,1)} %param.17) | copy-start | bytes 6291460
  32.8 0.9 copy-start.5
  33.7 0.7 copy-start.11
  36.3 15.3 %all-to-all-start = ((bf16[32,32,256]{2,1,0:T(8,128)(2,1)}), bf16[32,32,256]{2,1,0:T(8,128)(2,1)S(1)}, u32[]{:S(2)}, u32[]{:S(2)}) async-start(bf16[32,32,256]{2,1,0:T(8,128)(2,1)} %bitcast.15), calls=%async_computation | async-start | bytes 1048576 | tf_op jit(solution)/shard_map/all_to_all | solution.py:525
  41.3 1.6 %copy-start.1 = (bf16[1,1,64,2,32,256]{5,4,3,2,1,0:T(8,128)(2,1)S(1)}, bf16[1,1,64,2,32,256]{5,4,3,2,1,0:T(8,128)(2,1)}, u32[]{:S(2)}) copy-start(bf16[1,1,64,2,32,256]{5,4,3,2,1,0:T(8,128)(2,1)} %param.16) | copy-start | bytes 6291460
  42.9 0.8 copy-start.8
  43.7 0.7 copy-start.15
  44.4 13.6 %copy-start.6 = (bf16[2,192,256]{2,1,0:T(8,128)(2,1)S(1)}, bf16[2,192,256]{2,1,0:T(8,128)(2,1)}, u32[]{:S(2)}) copy-start(bf16[2,192,256]{2,1,0:T(8,128)(2,1)} %get-tuple-element.14.pb_ref.pb) | copy-start | bytes 589828
  44.4 13.6 %copy-start.12 = (s32[32,1,128]{2,1,0:T(1,128)S(1)}, s32[32,1,128]{2,1,0:T(1,128)}, u32[]{:S(2)}) copy-start(s32[32,1,128]{2,1,0:T(1,128)} %get-tuple-element.12) | copy-start | bytes 49156
  49.5 0.8 copy-start.3
  50.3 30.5 %copy-start.16 = (s32[1,1,64]{2,1,0:T(1,128)S(1)}, s32[1,1,64]{2,1,0:T(1,128)}, u32[]{:S(2)}) copy-start(s32[1,1,64]{2,1,0:T(1,128)} %param.15) | copy-start | bytes 772
  51.6 29.2 %all-to-all-start.1 = ((bf16[32,32,256]{2,1,0:T(8,128)(2,1)}), bf16[32,32,256]{2,1,0:T(8,128)(2,1)S(1)}, u32[]{:S(2)}, u32[]{:S(2)}) async-start(bf16[32,32,256]{2,1,0:T(8,128)(2,1)} %bitcast.33), calls=%async_computation.1 | async-start | bytes 1048576 | tf_op jit(solution)/shard_map/all_to_all | solution.py:521
  58.0 1.1 copy-start.4
  79.3 0.8 copy-start.7
  80.1 0.7 copy-start.9
  80.8 1.6 %copy-start.2 = (bf16[1,1,64,2,32,256]{5,4,3,2,1,0:T(8,128)(2,1)S(1)}, bf16[1,1,64,2,32,256]{5,4,3,2,1,0:T(8,128)(2,1)}, u32[]{:S(2)}) copy-start(bf16[1,1,64,2,32,256]{5,4,3,2,1,0:T(8,128)(2,1)} %param.16) | copy-start | bytes 6291460
  82.4 0.9 copy-start.10
  89.4 0.6 copy-start.13
  90.1 0.7 copy-start.14

commit v2 on v0

v2 whole, which is shorter than its diff:
```python
import jax
import jax.numpy as jnp
from jax import lax
from jax.experimental import pallas as pl
from jax.experimental.pallas import tpu as pltpu
from jax.sharding import Mesh, PartitionSpec as P

f32 = jnp.float32
bf16 = jnp.bfloat16
i32 = jnp.int32
MESH = pl.DeviceIdType.MESH
KF = 48


def rem(a, n):
    return lax.rem(a, jnp.int32(n))


def plane_peer(flat):
    return flat // 8, rem(flat // 4, 2), rem(flat, 4)


def split3(v):
    h = v.astype(bf16).astype(f32)
    m = (v - h).astype(bf16).astype(f32)
    return h, m, v - h - m


def feats(load, vref, left):
    xs = [load(128 + 16 * k).astype(f32) - 0.5 for k in range(3)]
    a = load(176).astype(f32)
    w = 256.0 / (a * a)
    n = (xs[0] * xs[0] + xs[1] * xs[1] + xs[2] * xs[2] + 0.005) * w
    rows = [n, w] if left else [w, n]
    rows += [v * ((-2.0 if left else 1.0) * w) for v in xs]
    for k, r in enumerate(rows):
        vref[0, pl.ds(k, 16, stride=8), :] = r[:, :128]
        vref[1, pl.ds(k, 16, stride=8), :] = r[:, 128:]


def rows8(vref, c):
    o = pl.ds(pl.multiple_of(8 * c, 8), 8)
    return jnp.concatenate([vref[0, o, :], vref[1, o, :]], 1)


def left_factor(v):
    h, m, l = split3(v)
    return jnp.concatenate([h, h, m, m, h, l], 0).astype(bf16)


def right_factor(v):
    h, m, l = split3(v)
    return jnp.concatenate([h, m, h, m, l, h], 0).T.astype(bf16)


def through(dens, first, second, mask):
    p = lax.dot_general(dens, first, (((1,), (1,)), ((), ())), preferred_element_type=f32)
    p = (p.astype(bf16).astype(f32) * mask).astype(bf16)
    return jnp.dot(p, second, preferred_element_type=f32)


def pick_matrix(ids, rows):
    lane = lax.broadcasted_iota(i32, (1, 256), 1)
    key = jnp.full((1, 256), -8, i32)
    for n, v in enumerate(ids):
        key = jnp.where(lane // 8 == n, v * 8, key)
    key = key + rem(lane, 8)
    return jnp.where(lax.broadcasted_iota(i32, (rows, 256), 0) == key, 1.0, 0.0).astype(bf16)


def gathered(sel, v):
    hi = v.astype(bf16)
    lo = (v - hi.astype(f32)).astype(bf16)
    return jnp.dot(sel, hi, preferred_element_type=f32) + jnp.dot(sel, lo, preferred_element_type=f32)


def kernel(near, ncnt, far, dens, pos, area, fars, fcnts, left_h, right_h, out,
           left, right, pack, pa, pb, t1, t2, isrc, igot, cvm, csm, vl, lf, rt, da, db, dself, ub, rbuf, cbuf,
           acc_b, own, fc, fcr, fd, fdr, sa, sb, ra, rb, part,
           lsem, s_a, r_a, s_b, r_b, s_i, r_i, s_fc, r_fc, s_fd, r_fd, s_oa, r_oa, s_ob, r_ob, s_o, r_o):
    z, x, c, y = (lax.axis_index(n) for n in ("z", "x", "c", "y"))
    row = x * 2 + c
    me = row * 4 + y
    owner = rem(z, 4) == y
    half = z // 4
    zy = rem(z, 4)

    def each(lo, hi, f):
        def body(t, _):
            f(t)
            return 0
        lax.fori_loop(lo, hi, body, 0)

    cl = pltpu.make_async_copy(left_h, left, lsem.at[0])
    cr = pltpu.make_async_copy(right_h, right, lsem.at[1])
    cl.start()
    cr.start()

    barrier = pltpu.get_barrier_semaphore()

    def greet(dev):
        pl.semaphore_signal(barrier, inc=1, device_id=dev, device_id_type=MESH)

    def plane_dev(q):
        px, pc, py = plane_peer(q)
        return (z, px, pc, py)

    each(1, 32, lambda t: greet(plane_dev(rem(me + t, 32))))
    each(1, 8, lambda t: greet((rem(z + t, 8), x, c, zy)))
    for h in range(2):
        @pl.when(z != h * 4 + y)
        def _(h=h):
            greet((h * 4 + y, x, c, y))

    pack[0:128, :] = dens[...]
    pack[128:176, :] = pos[...]
    pack[176:192, :] = area[...]
    t1[...] = jnp.zeros_like(t1)
    t2[...] = jnp.zeros_like(t2)
    t1[:, 0:64] = near[...]
    t2[0:1, 0:64] = ncnt[...]
    t2[1:2, 0:64] = far[1:2, :]
    t2[2:3, 0:64] = far[3:4, :]
    lane8 = lax.broadcasted_iota(i32, (8, 128), 1)
    isrc[...] = jnp.where(lane8 < 64, t1[...], pltpu.roll(t2[...], 64, 1))
    igot[me] = isrc[...]

    @pl.when(owner)
    def _():
        pb[half] = pack[...]
        pl.semaphore_wait(barrier, 42)

    @pl.when(jnp.logical_not(owner))
    def _():
        pl.semaphore_wait(barrier, 39)

    def remote(src, dst, ss, rs, dev):
        return pltpu.make_async_remote_copy(src_ref=src, dst_ref=dst, send_sem=ss, recv_sem=rs,
                                            device_id=dev, device_id_type=MESH)

    def copy_b(t, h):
        return remote(pack, pb.at[h], s_b.at[t], r_b.at[h], (rem(z + t, 8), x, c, y))

    @pl.when(owner)
    def _():
        each(1, 8, lambda t: copy_b(t, half).start())

    def copy_i(t, slot):
        return remote(isrc, igot.at[slot], s_i.at[t], r_i.at[slot], plane_dev(rem(me + t, 32)))

    each(1, 32, lambda t: copy_i(t, me).start())

    def copy_a(t, slot):
        p = rem(row + 8 - t, 8)
        return remote(pack, pa.at[slot], s_a.at[t], r_a.at[slot], (z, p // 2, rem(p, 2), y))

    each(1, 8, lambda t: copy_a(t, row).start())

    def tables(load, dref, base):
        for k in range(8):
            v = load(16 * k).astype(f32)
            dref[base + 2 * k] = v[:8]
            dref[base + 2 * k + 1] = v[8:]

    vl[...] = jnp.zeros_like(vl)
    tables(lambda o: pack[o:o + 16, :], da, 0)
    kr = lax.broadcasted_iota(i32, (64, 256), 0) // 8
    kc = lax.broadcasted_iota(i32, (64, 256), 1) // 32
    mask = jnp.where(kr == kc, 1.0, 0.0)

    def far_owner(q, h):
        return h * 32 + rem(q, 4) * 8 + q // 4

    def copy_fc(q, slot):
        return remote(fc.at[q], fcr.at[slot], s_fc.at[q], r_fc.at[slot], plane_dev(q))

    cl.wait()
    cr.wait()

    def far_cols(t):
        qs = [rem(me + 2 * t, 32), rem(me + 2 * t + 1, 32)]
        es = [far_owner(q, h) for q in qs for h in range(2)]
        ds = []
        for e in es:
            for k in range(2):
                i = rem(fars[2 * k, e], 16)
                ds.append(jnp.where(k < fcnts[0, e], da[i], 0.0))
        r = through(jnp.concatenate(ds, 0).astype(bf16), jnp.concatenate([left[e] for e in es], 0),
                    jnp.concatenate([right[e] for e in es], 0), mask).astype(bf16)
        fc[qs[0]] = r[:32]
        fc[qs[1]] = r[32:]

        @pl.when(t > 0)
        def _():
            copy_fc(qs[0], me).start()

        copy_fc(qs[1], me).start()

    each(0, 16, far_cols)
    fcr[me] = fc[me]

    def prep(load, par):
        feats(load, vl, True)
        for k in range(16):
            lf[par * 16 + k] = left_factor(rows8(vl, k))
        tables(load, da, par * 16)

    prep(lambda o: pack[o:o + 16, :], 0)
    feats(lambda o: pack[o:o + 16, :], vl, False)
    own[...] = jnp.zeros_like(own)
    for s in range(4):
        k = 4 * y + s
        u = lax.rsqrt(jnp.dot(right_factor(rows8(vl, k)), lf[k], preferred_element_type=f32)).astype(bf16)
        own[pl.ds(pl.multiple_of(8 * k, 8), 8), :] = jnp.dot(da[k].astype(bf16), u, preferred_element_type=f32)

    each(1, 32, lambda t: copy_i(t, rem(me + t, 32)).wait_recv())
    q0 = y * 8 + row
    lists = jnp.zeros((8, 128), i32)
    for s in range(32):
        lists = jnp.where(rem(lane8, 32) == s, pltpu.roll(igot[s], rem(s - q0 + 128, 128), 1), lists)
    cvm[...] = lists
    ci = pltpu.make_async_copy(cvm, csm, lsem.at[0])
    ci.start()
    for h in range(2):
        @pl.when(z != h * 4 + y)
        def _(h=h):
            copy_b(1, h).wait_recv()
    for h in range(2):
        feats(lambda o, h=h: pb[h, o:o + 16, :], vl, False)
        for k in range(16):
            rt[h * 16 + k] = right_factor(rows8(vl, k))
        tables(lambda o, h=h: pb[h, o:o + 16, :], db, h * 16)
    ci.wait()

    def far_col(s, h, k):
        return h * 16 + rem(csm[1 + k, 64 + h * 32 + s], 16)

    def copy_fd(s, slot):
        return remote(fd.at[s], fdr.at[slot], s_fd.at[s], r_fd.at[slot], plane_dev(s))

    def send_fd(t):
        s = rem(me + t, 32)
        fd[s] = jnp.concatenate([db[far_col(s, h, k)] for h in range(2) for k in range(2)], 0).astype(bf16)

        @pl.when(t > 0)
        def _():
            copy_fd(s, me).start()

    each(0, 32, send_fd)
    fdr[me] = fd[me]

    def slot_ids(b, n):
        s, h, k = 4 * b + n // 8, (n // 4) % 2, n % 4
        return (rem(csm[2 * k, h * 32 + s], 16), h * 16 + rem(csm[2 * k + 1, h * 32 + s], 16),
                k < csm[0, 64 + h * 32 + s])

    def build(b, par, first, slot):
        for g in range(16):
            i, j, _ = slot_ids(b, first + g)
            d2 = jnp.dot(rt[j], lf[par * 16 + i], preferred_element_type=f32)
            ub[slot, g] = lax.rsqrt(d2).astype(bf16)

    def apply(b, par, first, slot):
        for g in range(16):
            n = first + g
            i, j, _ = slot_ids(b, n)
            u = ub[slot, g]
            rbuf[8 * n:8 * n + 8, :] = jnp.dot(db[j].astype(bf16), u, preferred_element_type=f32)
            cbuf[8 * n:8 * n + 8, :] = lax.dot_general(
                da[par * 16 + i].astype(bf16), u, (((1,), (1,)), ((), ())), preferred_element_type=f32)

    def copy_oa(b, yy, slot):
        return remote(sa.at[b, pl.ds(pl.multiple_of(yy * 32, 32), 32)], ra.at[slot], s_oa.at[b * 4 + yy], r_oa.at[slot],
                      (z, b // 2, rem(b, 2), yy))

    def sums(b):
        ids = [slot_ids(b, n) for n in range(32)]
        a = gathered(pick_matrix([jnp.where(v[2], v[0], -1) for v in ids], 128), rbuf[...])
        acc_b[...] += gathered(pick_matrix([jnp.where(v[2], v[1], -1) for v in ids], 256), cbuf[...])
        return a

    def finish(b):
        sa[b] = sums(b).astype(bf16)
        each(0, 4, lambda v: copy_oa(b, rem(y + v, 4), me).start())

    acc_b[...] = jnp.zeros_like(acc_b)
    build(row, 0, 0, 0)

    def group(t):
        b = rem(row + t, 8)
        nb = rem(row + t + 1, 8)
        par = rem(t, 2)
        copy_a(t + 1, nb).wait_recv()
        apply(b, par, 0, 0)
        build(b, par, 16, 1)
        prep(lambda o: pa[nb, o:o + 16, :], 1 - par)
        apply(b, par, 16, 1)
        build(nb, 1 - par, 0, 0)

        @pl.when(t == 0)
        def _():
            own[...] += sums(b)

        @pl.when(t > 0)
        def _():
            finish(b)

    each(0, 7, group)
    last = rem(row + 7, 8)
    apply(last, 1, 0, 0)
    build(last, 1, 16, 1)
    apply(last, 1, 16, 1)
    finish(last)

    def wait_fc(t):
        q = rem(me + t, 32)
        copy_fc(q, q).wait_recv()

    each(1, 32, wait_fc)

    def add_cols(g):
        ids = [far_col(g * 8 + n // 4, (n // 2) % 2, n % 2) for n in range(32)]
        v = jnp.concatenate([fcr[g * 8 + k] for k in range(8)], 0)
        acc_b[...] += jnp.dot(pick_matrix(ids, 256), v, preferred_element_type=f32)

    each(0, 4, add_cols)
    for h in range(2):
        sb[h] = acc_b[128 * h:128 * h + 128, :].astype(bf16)

    def copy_ob(h, yy, slot):
        return remote(sb.at[h, pl.ds(pl.multiple_of(yy * 32, 32), 32)], rb.at[slot], s_ob.at[h * 4 + yy], r_ob.at[slot],
                      (h * 4 + y, x, c, yy))

    def all_ob(f):
        for h in range(2):
            for v in range(4):
                yy = rem(y + v, 4)
                if v == 0:
                    @pl.when(z != h * 4 + y)
                    def _(h=h, yy=yy):
                        f(copy_ob(h, yy, z))
                else:
                    f(copy_ob(h, yy, z))

    all_ob(lambda cp: cp.start())

    @pl.when(owner)
    def _():
        rb[z] = sb[half, pl.ds(pl.multiple_of(y * 32, 32), 32), :]

    def wait_fd(t):
        q = rem(me + t, 32)
        copy_fd(q, q).wait_recv()

    each(1, 32, wait_fd)

    def far_rows(g):
        ids = []
        for b in range(4):
            qs = [g * 8 + 2 * b, g * 8 + 2 * b + 1]
            es = [far_owner(q, h) for q in qs for h in range(2)]
            rbuf[64 * b:64 * b + 64, :] = through(
                jnp.concatenate([fdr[q] for q in qs], 0), jnp.concatenate([right[e] for e in es], 0),
                jnp.concatenate([left[e] for e in es], 0), mask)
            ids += [jnp.where(k < fcnts[0, e], rem(fars[2 * k, e], 16), -1) for e in es for k in range(2)]
        own[...] += gathered(pick_matrix(ids, 128), rbuf[...])

    each(0, 4, far_rows)

    sa[row] = own[...].astype(bf16)
    each(1, 4, lambda v: copy_oa(row, rem(y + v, 4), me).start())
    part[...] = own[pl.ds(pl.multiple_of(y * 32, 32), 32), :]

    def add_a(t):
        q = rem(me + t, 32)
        copy_oa(row, y, q).wait_recv()
        part[...] += ra[q].astype(f32)

    each(1, 32, add_a)

    def add_b(t):
        s = rem(z + t, 8)

        @pl.when(jnp.logical_not(owner & (s == z)))
        def _():
            copy_ob(half, y, s).wait_recv()

        part[...] += rb[s].astype(f32)

    each(0, 8, add_b)

    def copy_o(t, slot):
        return remote(part, out.at[pl.ds(pl.multiple_of(slot * 32, 32), 32)], s_o.at[t], r_o.at[slot],
                      (z, x, c, rem(y + t, 4)))

    each(1, 4, lambda t: copy_o(t, y).start())
    out[pl.ds(pl.multiple_of(y * 32, 32), 32), :] = part[...]

    def sent_plane(t):
        q = rem(me + t, 32)
        copy_i(t, me).wait_send()
        copy_fc(q, me).wait_send()
        copy_fd(q, me).wait_send()

    each(1, 32, sent_plane)
    each(1, 8, lambda t: copy_a(t, row).wait_send())

    @pl.when(owner)
    def _():
        each(1, 8, lambda t: copy_b(t, half).wait_send())

    def sent_oa(t):
        b = rem(row + t, 8)
        each(0, 4, lambda v: copy_oa(b, rem(y + v, 4), me).wait_send())

    each(1, 8, sent_oa)
    each(1, 4, lambda v: copy_oa(row, rem(y + v, 4), me).wait_send())
    all_ob(lambda cp: cp.wait_send())
    each(1, 4, lambda t: copy_o(t, rem(y + t, 4)).wait_recv())
    each(1, 4, lambda t: copy_o(t, y).wait_send())


def per_device(density, positions, areas, near_pairs, near_counts, far_pairs, far_counts, far_right, far_left):
    near = near_pairs[0, 0].transpose(1, 2, 0).reshape(8, 64)
    far = far_pairs[0, 0].transpose(1, 2, 0).reshape(4, 64)
    ncnt = near_counts.reshape(1, 64)
    fcnt = far_counts.reshape(1, 64)
    left = far_left.reshape(64, 64, 256)
    right = far_right.reshape(64, 64, 256)
    vm = pl.BlockSpec(memory_space=pltpu.VMEM)
    sm = pl.BlockSpec(memory_space=pltpu.SMEM)
    hbm = pl.BlockSpec(memory_space=pl.ANY)
    V, D = pltpu.VMEM, pltpu.SemaphoreType.DMA
    out = pl.pallas_call(
        kernel,
        out_shape=jax.ShapeDtypeStruct((128, 256), f32),
        in_specs=[vm] * 6 + [sm] * 2 + [hbm] * 2,
        out_specs=vm,
        scratch_shapes=[
            V((64, 64, 256), bf16), V((64, 64, 256), bf16), V((192, 256), bf16), V((8, 192, 256), bf16),
            V((2, 192, 256), bf16), V((8, 128), i32), V((8, 128), i32), V((8, 128), i32), V((32, 8, 128), i32),
            V((8, 128), i32), pltpu.SMEM((8, 128), i32), V((2, 128, 128), f32), V((32, KF, 256), bf16),
            V((32, 256, KF), bf16), V((32, 8, 256), f32), V((32, 8, 256), f32), V((16, 8, 256), f32),
            V((2, 16, 256, 256), bf16), V((256, 256), f32), V((256, 256), f32),
            V((256, 256), f32), V((128, 256), f32), V((32, 32, 256), bf16), V((32, 32, 256), bf16),
            V((32, 32, 256), bf16), V((32, 32, 256), bf16), V((8, 128, 256), bf16), V((2, 128, 256), bf16),
            V((32, 32, 256), bf16), V((8, 32, 256), bf16), V((32, 256), f32),
            D((2,)), D((8,)), D((8,)), D((8,)), D((2,)), D((32,)), D((32,)), D((32,)), D((32,)), D((32,)), D((32,)),
            D((32,)), D((32,)), D((8,)), D((8,)), D((4,)), D((4,)),
        ],
        compiler_params=pltpu.CompilerParams(collective_id=1, has_side_effects=True,
                                             vmem_limit_bytes=56 * 1024 * 1024),
    )(near, ncnt, far, density.reshape(128, 256), positions.transpose(1, 0, 2).reshape(48, 256), areas,
      far, fcnt, left, right)
    return out.reshape(16, 8, 256)


def solution(mesh):
    grid = Mesh(mesh.devices.reshape(8, 4, 2, 4), ("z", "x", "c", "y"))
    d = ("z", "x", "c")
    return jax.shard_map(
        per_device,
        mesh=grid,
        in_specs=(
            P(d, None, None),
            P(d, None, None),
            P(d, None),
            P(d, "y", None, None, None),
            P(d, "y", None),
            P(d, "y", None, None, None),
            P(d, "y", None),
            P(d, "y", None, None, None, None),
            P(d, "y", None, None, None, None),
        ),
        out_specs=P(d, None, None),
        check_vma=False,
    )
```

time: 634 us -> 71.2 us (0.11)
  waiting for transfers between devices: 300 us -> 0 us
  matrix products: 196 us -> 0 us
  Pallas kernels: 0 us -> 69 us
  blocking collectives: 54.8 us -> 0 us
  local copies, waits for them, and re-layouts: 37.5 us -> 1.57 us
  other arithmetic: 21 us -> 0 us
  between operations: 13.5 us -> 0.01 us
  starting transfers between devices: 6.68 us -> 0 us
    dot_general x22 -> x0, matrix products: 196 us -> none  [the longest x8 103 us: near_block(): jnp.einsum('tab,trb->tra', tile_set, dens_col, preferred_element_type=jnp...]
    all_to_all x1 -> x0, waiting for transfers between devices: 176 us -> none  [per_device(): lax.all_to_all(reduced_sum, 'clus', split_axis=0, concat_axis=0, tiled=True)]
    all_gather x2 -> x0, waiting for transfers between devices: 77.5 us -> none  [the longest x1 73.1 us: per_device(): lax.all_gather(density, 'clus', axis=0, tiled=True)]
    pallas_call x0 -> x1, Pallas kernels: none -> 69 us  [per_device(): pl.pallas_call(kernel, out_shape=jax.ShapeDtypeStruct((128, 256), f32), i...]
    all_gather x1 -> x0, blocking collectives: 54.8 us -> none  [per_device(): lax.all_gather(areas, 'clus', axis=0, tiled=True)]
    psum x1 -> x0, waiting for transfers between devices: 45.1 us -> none  [per_device(): return lax.psum(partial_value, 'rep')]
    gather x8 -> x0, local copies, waits for them, and re-layouts: 17.9 us -> none  [the longest x1 4.2 us: per_device(): got_dens = all_dens[global_ids]]
    convert_element_type x22 -> x0, other arithmetic: 13.4 us -> none  [the longest x9 6.52 us: build(): right_pos = right_pos.astype(jnp.float32)]
  transfers between devices with their start and end apart: 4 -> 0, of which waited for: 4 -> 0; matrix products, arithmetic and copies ran while one was open for 5% -> 0% of each run, Pallas kernels for 0% -> 0%
where the time goes in v2:
time: 71.2 us; the launch traced here: 70.6 us
  Pallas kernels  69 us (97%)
  local copies, waits for them, and re-layouts  1.57 us (2%)
    pallas_call x1, Pallas kernels, per_device(): pl.pallas_call(kernel, out_shape=jax.ShapeDtypeStruct((128, 256), f32), i...  69 us
    unnamed x1, local copies, waits for them, and re-layouts  1.57 us

profile of v2, /device:TPU:1, one launch (start us, length us, event | category | flops | bytes accessed | tf_op | source)
XLA Modules:
  0.0 70.6 jit_solution(5874512855991990985)
XLA Ops:
  0.0 69.0 %shard_map.91 = f32[128,256]{1,0:T(8,128)} custom-call(s32[8,64]{1,0:T(8,128)} %bitcast.26, s32[1,64]{1,0:T(1,128)} %bitcast.27, s32[4,64]{1,0:T(4,128)} %bitcast.24, bf16[128,256]{1,0:T(8,128)(2,1)} %bitcast.22, bf16[48,256]{1,0:T(8,128)(2,1)} %bitcast.23, bf16[16,256]{1,0:T(8,128)(2,1)} %area.1, s32[4,64]{1,0:T(4,128)} %bitcast.25, s32[1,64]{1,0:T(1,128)} %bitcast.28, ...), custom_call_target="tpu_custom_call" | custom-call | tf_op jit(solution)/shard_map/pallas_call | solution.py:434
  69.0 1.6 %copy.11 = f32[16,8,256]{2,1,0:T(8,128)} copy(f32[16,8,256]{2,1,0:T(8,128)} %bitcast.21) | data formatting | bytes 262144

commit v3 on v2

v3 whole, which is shorter than its diff:
```python
import jax
import jax.numpy as jnp
from jax import lax
from jax.experimental import pallas as pl
from jax.experimental.pallas import tpu as pltpu
from jax.sharding import Mesh, PartitionSpec as P

f32 = jnp.float32
bf16 = jnp.bfloat16
i32 = jnp.int32
MESH = pl.DeviceIdType.MESH
KF = 48


def rem(a, n):
    return lax.rem(a, jnp.int32(n))


def plane_peer(flat):
    return flat // 8, rem(flat // 4, 2), rem(flat, 4)


def split3(v):
    h = v.astype(bf16).astype(f32)
    m = (v - h).astype(bf16).astype(f32)
    return h, m, v - h - m


def feats(load, vref, left):
    xs = [load(128 + 16 * k).astype(f32) - 0.5 for k in range(3)]
    a = load(176).astype(f32)
    w = 256.0 / (a * a)
    n = (xs[0] * xs[0] + xs[1] * xs[1] + xs[2] * xs[2] + 0.005) * w
    rows = [n, w] if left else [w, n]
    rows += [v * ((-2.0 if left else 1.0) * w) for v in xs]
    for k, r in enumerate(rows):
        vref[0, pl.ds(k, 16, stride=8), :] = r[:, :128]
        vref[1, pl.ds(k, 16, stride=8), :] = r[:, 128:]


def rows8(vref, c):
    o = pl.ds(pl.multiple_of(8 * c, 8), 8)
    return jnp.concatenate([vref[0, o, :], vref[1, o, :]], 1)


def left_factor(v):
    h, m, l = split3(v)
    return jnp.concatenate([h, h, m, m, h, l], 0).astype(bf16)


def right_factor(v):
    h, m, l = split3(v)
    return jnp.concatenate([h, m, h, m, l, h], 0).T.astype(bf16)


def through(dens, first, second, mask):
    p = lax.dot_general(dens, first, (((1,), (1,)), ((), ())), preferred_element_type=f32)
    p = (p.astype(bf16).astype(f32) * mask).astype(bf16)
    return jnp.dot(p, second, preferred_element_type=f32)


def pick_matrix(ids, rows):
    lane = lax.broadcasted_iota(i32, (1, 256), 1)
    key = jnp.full((1, 256), -8, i32)
    for n, v in enumerate(ids):
        key = jnp.where(lane // 8 == n, v * 8, key)
    key = key + rem(lane, 8)
    return jnp.where(lax.broadcasted_iota(i32, (rows, 256), 0) == key, 1.0, 0.0).astype(bf16)


def gathered(sel, v):
    hi = v.astype(bf16)
    lo = (v - hi.astype(f32)).astype(bf16)
    return jnp.dot(sel, hi, preferred_element_type=f32) + jnp.dot(sel, lo, preferred_element_type=f32)


def kernel(near, ncnt, far, dens, pos, area, fars, fcnts, left_h, right_h, out,
           left, right, pack, pa, pb, t1, t2, igy, igot, cvm, csm, vl, lf, rt, da, db, ub, rbuf, cbuf,
           acc_b, own, fc, fcy, fcr, fd, fdy, fdr, sa, sb, ra, rb, part,
           lsem, s_a, r_a, s_b, r_b, s_y, r_y, s_r, r_r, s_oa, r_oa, s_ob, r_ob, s_o, r_o):
    z, x, c, y = (lax.axis_index(n) for n in ("z", "x", "c", "y"))
    row = x * 2 + c
    me = row * 4 + y
    half = z // 4
    zy = rem(z, 4)
    owner = zy == y

    def each(lo, hi, f):
        def body(t, _):
            f(t)
            return 0
        lax.fori_loop(lo, hi, body, 0)

    cl = pltpu.make_async_copy(left_h, left, lsem.at[0])
    cr = pltpu.make_async_copy(right_h, right, lsem.at[1])
    cl.start()
    cr.start()

    barrier = pltpu.get_barrier_semaphore()

    def greet(dev):
        pl.semaphore_signal(barrier, inc=1, device_id=dev, device_id_type=MESH)

    def plane_dev(q):
        px, pc, py = plane_peer(q)
        return (z, px, pc, py)

    each(1, 32, lambda t: greet(plane_dev(rem(me + t, 32))))
    each(1, 8, lambda t: greet((rem(z + t, 8), x, c, zy)))
    for h in range(2):
        @pl.when(z != h * 4 + y)
        def _(h=h):
            for v in range(4):
                greet((h * 4 + y, x, c, v))

    pack[0:128, :] = dens[...]
    pack[128:176, :] = pos[...]
    pack[176:192, :] = area[...]
    t1[...] = jnp.zeros_like(t1)
    t2[...] = jnp.zeros_like(t2)
    t1[:, 0:64] = near[...]
    t2[0:1, 0:64] = ncnt[...]
    t2[1:2, 0:64] = far[1:2, :]
    t2[2:3, 0:64] = far[3:4, :]
    lane8 = lax.broadcasted_iota(i32, (8, 128), 1)
    igy[y] = jnp.where(lane8 < 64, t1[...], pltpu.roll(t2[...], 64, 1))

    def quarter(n):
        return pl.ds(pl.multiple_of(y * n, n), n)

    @pl.when(owner)
    def _():
        pb[half, quarter(48), :] = pack[quarter(48), :]
        pl.semaphore_wait(barrier, 42)

    @pl.when(jnp.logical_not(owner))
    def _():
        pl.semaphore_wait(barrier, 46)

    def remote(src, dst, ss, rs, dev):
        return pltpu.make_async_remote_copy(src_ref=src, dst_ref=dst, send_sem=ss, recv_sem=rs,
                                            device_id=dev, device_id_type=MESH)

    side = (z, x, c, rem(y + 1, 4))

    def copy_b(t):
        return remote(pack.at[quarter(48)], pb.at[half, quarter(48)], s_b, r_b.at[half], (rem(z + t, 8), x, c, zy))

    for t in (4, 3, 5, 2, 6, 1, 7):
        copy_b(t).start()

    @pl.when(jnp.logical_not(owner))
    def _():
        copy_b(0).start()

    def step_y(src, dst, k):
        for t in range(1, 4):
            yy = rem(y + t, 4)
            remote(src(yy), dst.at[y], s_y.at[k], r_y.at[k], (z, x, c, yy)).start()

    def wait_y(dst, k):
        w = dst.at[pl.ds(0, 3)]
        remote(w, w, s_y.at[k], r_y.at[k], side).wait_recv()

    def step_row(src, dst, k):
        def one(t):
            p = rem(row + 8 - t, 8)
            remote(src.at[:, p], dst.at[row], s_r.at[k], r_r.at[k], (z, p // 2, rem(p, 2), y)).start()
        each(1, 8, one)

    def wait_row(dst, k):
        w = dst.at[pl.ds(0, 7)]
        remote(w, w, s_r.at[k], r_r.at[k], side).wait_recv()

    step_y(lambda yy: igy.at[y], igy, 0)

    def copy_a(t, slot):
        p = rem(row + 8 - t, 8)
        return remote(pack, pa.at[slot], s_a, r_a.at[slot], (z, p // 2, rem(p, 2), y))

    def tables(load, dref, base):
        for k in range(8):
            v = load(16 * k).astype(f32)
            dref[base + 2 * k] = v[:8]
            dref[base + 2 * k + 1] = v[8:]

    def prep(load, par):
        feats(load, vl, True)
        for k in range(16):
            lf[par * 16 + k] = left_factor(rows8(vl, k))
        tables(load, da, par * 16)

    vl[...] = jnp.zeros_like(vl)
    prep(lambda o: pack[o:o + 16, :], 0)
    feats(lambda o: pack[o:o + 16, :], vl, False)
    own[...] = jnp.zeros_like(own)
    for s in range(4):
        k = 4 * y + s
        u = lax.rsqrt(jnp.dot(right_factor(rows8(vl, k)), lf[k], preferred_element_type=f32)).astype(bf16)
        own[pl.ds(pl.multiple_of(8 * k, 8), 8), :] = jnp.dot(da[k].astype(bf16), u, preferred_element_type=f32)

    kr = lax.broadcasted_iota(i32, (64, 256), 0) // 8
    kc = lax.broadcasted_iota(i32, (64, 256), 1) // 32
    mask = jnp.where(kr == kc, 1.0, 0.0)

    def far_owner(p, yy, h):
        return h * 32 + yy * 8 + p

    def far_cols(p):
        for v in range(2):
            es = [far_owner(p, yy, h) for yy in (2 * v, 2 * v + 1) for h in range(2)]
            ds = []
            for e in es:
                for k in range(2):
                    i = rem(fars[2 * k, e], 16)
                    ds.append(jnp.where(k < fcnts[0, e], da[i], 0.0))
            r = through(jnp.concatenate(ds, 0).astype(bf16), jnp.concatenate([left[e] for e in es], 0),
                        jnp.concatenate([right[e] for e in es], 0), mask).astype(bf16)
            fc[2 * v, p] = r[:32]
            fc[2 * v + 1, p] = r[32:]

    cl.wait()
    cr.wait()
    each(0, 4, far_cols)

    wait_y(igy, 0)
    own_i = pltpu.make_async_copy(igy, igot.at[row], lsem.at[0])
    own_i.start()

    def send_i(t):
        p = rem(row + 8 - t, 8)
        remote(igy, igot.at[row], s_r.at[0], r_r.at[0], (z, p // 2, rem(p, 2), y)).start()

    each(1, 8, send_i)
    each(4, 8, far_cols)
    step_y(lambda yy: fc.at[yy], fcy, 1)
    own_c = pltpu.make_async_copy(fc.at[y], fcy.at[y], lsem.at[1])
    own_c.start()

    each(1, 8, lambda t: copy_a(t, row).start())

    own_i.wait()
    wait_row(igot, 0)
    q0 = y * 8 + row
    lists = jnp.zeros((8, 128), i32)
    for s in range(32):
        lists = jnp.where(rem(lane8, 32) == s, pltpu.roll(igot[s // 4, s % 4], rem(s - q0 + 128, 128), 1), lists)
    cvm[...] = lists
    ci = pltpu.make_async_copy(cvm, csm, lsem.at[2])
    ci.start()
    for h in range(2):
        w4 = pb.at[h]
        w3 = pb.at[h, pl.ds(0, 144)]

        @pl.when(z != h * 4 + y)
        def _(w4=w4, h=h):
            remote(w4, w4, s_b, r_b.at[h], side).wait_recv()

        @pl.when(z == h * 4 + y)
        def _(w3=w3, h=h):
            remote(w3, w3, s_b, r_b.at[h], side).wait_recv()

    for h in range(2):
        feats(lambda o, h=h: pb[h, o:o + 16, :], vl, False)
        for k in range(16):
            rt[h * 16 + k] = right_factor(rows8(vl, k))
        tables(lambda o, h=h: pb[h, o:o + 16, :], db, h * 16)
    ci.wait()

    def far_col(s, h, k):
        return h * 16 + rem(csm[1 + k, 64 + h * 32 + s], 16)

    def fill_fd(p):
        for yy in range(4):
            s = p * 4 + yy
            fd[yy, p] = jnp.concatenate([db[far_col(s, h, k)] for h in range(2) for k in range(2)], 0).astype(bf16)

    each(0, 8, fill_fd)
    own_c.wait()
    own_d = pltpu.make_async_copy(fd.at[y], fdy.at[y], lsem.at[0])
    own_d.start()
    step_y(lambda yy: fd.at[yy], fdy, 2)
    own_d.wait()

    def slot_ids(b, n):
        s, h, k = 4 * b + n // 8, (n // 4) % 2, n % 4
        return (rem(csm[2 * k, h * 32 + s], 16), h * 16 + rem(csm[2 * k + 1, h * 32 + s], 16),
                k < csm[0, 64 + h * 32 + s])

    def build(b, par, first, slot):
        for g in range(16):
            i, j, _ = slot_ids(b, first + g)
            d2 = jnp.dot(rt[j], lf[par * 16 + i], preferred_element_type=f32)
            ub[slot, g] = lax.rsqrt(d2).astype(bf16)

    def apply(b, par, first, slot, rows=True, cols=True):
        for g in range(16):
            n = first + g
            i, j, _ = slot_ids(b, n)
            u = ub[slot, g]
            if rows:
                rbuf[8 * n:8 * n + 8, :] = jnp.dot(db[j].astype(bf16), u, preferred_element_type=f32)
            if cols:
                cbuf[8 * n:8 * n + 8, :] = lax.dot_general(
                    da[par * 16 + i].astype(bf16), u, (((1,), (1,)), ((), ())), preferred_element_type=f32)

    def copy_oa(b, yy, slot):
        return remote(sa.at[b, pl.ds(pl.multiple_of(yy * 32, 32), 32)], ra.at[slot], s_oa, r_oa,
                      (z, b // 2, rem(b, 2), yy))

    def row_sums(b):
        ids = [slot_ids(b, n) for n in range(32)]
        return gathered(pick_matrix([jnp.where(v[2], v[0], -1) for v in ids], 128), rbuf[...])

    def col_sums(b):
        ids = [slot_ids(b, n) for n in range(32)]
        acc_b[...] += gathered(pick_matrix([jnp.where(v[2], v[1], -1) for v in ids], 256), cbuf[...])

    def send_oa(b):
        for v in range(4):
            copy_oa(b, rem(y + v, 4), me).start()

    acc_b[...] = jnp.zeros_like(acc_b)
    build(row, 0, 0, 0)

    def group(t):
        b = rem(row + t, 8)
        nb = rem(row + t + 1, 8)
        par = rem(t, 2)
        copy_a(t + 1, nb).wait_recv()
        apply(b, par, 0, 0)
        build(b, par, 16, 1)
        prep(lambda o: pa[nb, o:o + 16, :], 1 - par)
        apply(b, par, 16, 1)
        build(nb, 1 - par, 0, 0)
        col_sums(b)
        sums = row_sums(b)

        @pl.when(t == 0)
        def _():
            own[...] += sums
            wait_y(fcy, 1)
            step_row(fcy, fcr, 1)

        @pl.when(t > 0)
        def _():
            sa[b] = sums.astype(bf16)
            send_oa(b)

        @pl.when(t == 2)
        def _():
            wait_y(fdy, 2)
            step_row(fdy, fdr, 2)

    each(0, 7, group)

    own_c2 = pltpu.make_async_copy(fcy.at[:, row], fcr.at[row], lsem.at[0])
    own_c2.start()
    own_d2 = pltpu.make_async_copy(fdy.at[:, row], fdr.at[row], lsem.at[1])
    own_d2.start()
    own_c2.wait()
    own_d2.wait()
    wait_row(fcr, 1)
    for g in range(4):
        ids = [far_col(g * 8 + n // 4, (n // 2) % 2, n % 2) for n in range(32)]
        v = jnp.concatenate([fcr[g * 2 + k // 4, k % 4] for k in range(8)], 0)
        acc_b[...] += jnp.dot(pick_matrix(ids, 256), v, preferred_element_type=f32)

    last = rem(row + 7, 8)
    apply(last, 1, 0, 0, rows=False)
    build(last, 1, 16, 1)
    apply(last, 1, 16, 1, rows=False)
    col_sums(last)
    for h in range(2):
        sb[h] = acc_b[128 * h:128 * h + 128, :].astype(bf16)

    def copy_ob(h, yy):
        return remote(sb.at[h, pl.ds(pl.multiple_of(yy * 32, 32), 32)], rb.at[z], s_ob, r_ob, (h * 4 + y, x, c, yy))

    for v in (1, 2, 3, 0):
        for h in range(2):
            if v == 0:
                @pl.when(z != h * 4 + y)
                def _(h=h):
                    copy_ob(h, y).start()
            else:
                copy_ob(h, rem(y + v, 4)).start()

    @pl.when(owner)
    def _():
        rb[z] = sb[half, quarter(32), :]

    apply(last, 1, 0, 0, cols=False)
    apply(last, 1, 16, 1, cols=False)
    sa[last] = row_sums(last).astype(bf16)
    send_oa(last)

    wait_row(fdr, 2)

    def far_rows(g):
        ids = []
        for b in range(4):
            p, yys = g * 2 + b // 2, (2 * (b % 2), 2 * (b % 2) + 1)
            es = [far_owner(p, yy, h) for yy in yys for h in range(2)]
            rbuf[64 * b:64 * b + 64, :] = through(
                jnp.concatenate([fdr[p, yy] for yy in yys], 0), jnp.concatenate([right[e] for e in es], 0),
                jnp.concatenate([left[e] for e in es], 0), mask)
            ids += [jnp.where(k < fcnts[0, e], rem(fars[2 * k, e], 16), -1) for e in es for k in range(2)]
        own[...] += gathered(pick_matrix(ids, 128), rbuf[...])

    each(0, 4, far_rows)

    sa[row] = own[...].astype(bf16)
    for v in range(1, 4):
        copy_oa(row, rem(y + v, 4), me).start()
    ra[me] = jnp.zeros((32, 256), bf16)
    part[...] = own[quarter(32), :]
    w = ra.at[pl.ds(0, 31)]
    remote(w, w, s_oa, r_oa, side).wait_recv()

    def add_a(t):
        part[...] += ((ra[4 * t].astype(f32) + ra[4 * t + 1].astype(f32))
                      + (ra[4 * t + 2].astype(f32) + ra[4 * t + 3].astype(f32)))

    each(0, 8, add_a)

    def both(f):
        @pl.when(owner)
        def _():
            f(rb.at[pl.ds(0, 7)])

        @pl.when(jnp.logical_not(owner))
        def _():
            f(rb)

    both(lambda v: remote(v, v, s_ob, r_ob, side).wait_recv())
    part[...] += (((rb[0].astype(f32) + rb[1].astype(f32)) + (rb[2].astype(f32) + rb[3].astype(f32)))
                  + ((rb[4].astype(f32) + rb[5].astype(f32)) + (rb[6].astype(f32) + rb[7].astype(f32))))

    for t in range(1, 4):
        remote(part, out.at[quarter(32)], s_o, r_o, (z, x, c, rem(y + t, 4))).start()
    out[quarter(32), :] = part[...]

    both(lambda v: remote(v, v, s_ob, r_ob, side).wait_send())
    remote(w, w, s_oa, r_oa, side).wait_send()
    w = pa.at[pl.ds(0, 7)]
    remote(w, w, s_a, r_a.at[0], side).wait_send()
    for k, (vy, vr) in enumerate(((igy, igot), (fcy, fcr), (fdy, fdr))):
        w = vy.at[pl.ds(0, 3)]
        remote(w, w, s_y.at[k], r_y.at[k], side).wait_send()
        w = vr.at[pl.ds(0, 7)]
        remote(w, w, s_r.at[k], r_r.at[k], side).wait_send()
    w = pa.at[0, pl.ds(0, 48)]
    n_b = 7

    def sent_b(t):
        remote(w, w, s_b, r_b.at[0], side).wait_send()

    each(0, n_b, sent_b)

    @pl.when(jnp.logical_not(owner))
    def _():
        sent_b(0)

    w = out.at[pl.ds(0, 96)]
    remote(w, w, s_o, r_o, side).wait_recv()
    remote(w, w, s_o, r_o, side).wait_send()


def per_device(density, positions, areas, near_pairs, near_counts, far_pairs, far_counts, far_right, far_left):
    near = near_pairs[0, 0].transpose(1, 2, 0).reshape(8, 64)
    far = far_pairs[0, 0].transpose(1, 2, 0).reshape(4, 64)
    ncnt = near_counts.reshape(1, 64)
    fcnt = far_counts.reshape(1, 64)
    left = far_left.reshape(64, 64, 256)
    right = far_right.reshape(64, 64, 256)
    vm = pl.BlockSpec(memory_space=pltpu.VMEM)
    sm = pl.BlockSpec(memory_space=pltpu.SMEM)
    hbm = pl.BlockSpec(memory_space=pl.ANY)
    V, D = pltpu.VMEM, pltpu.SemaphoreType.DMA
    out = pl.pallas_call(
        kernel,
        out_shape=jax.ShapeDtypeStruct((128, 256), f32),
        in_specs=[vm] * 6 + [sm] * 2 + [hbm] * 2,
        out_specs=vm,
        scratch_shapes=[
            V((64, 64, 256), bf16), V((64, 64, 256), bf16), V((192, 256), bf16), V((8, 192, 256), bf16),
            V((2, 192, 256), bf16), V((8, 128), i32), V((8, 128), i32), V((4, 8, 128), i32), V((8, 4, 8, 128), i32),
            V((8, 128), i32), pltpu.SMEM((8, 128), i32), V((2, 128, 128), f32), V((32, KF, 256), bf16),
            V((32, 256, KF), bf16), V((32, 8, 256), f32), V((32, 8, 256), f32),
            V((2, 16, 256, 256), bf16), V((256, 256), f32), V((256, 256), f32), V((256, 256), f32), V((128, 256), f32),
            V((4, 8, 32, 256), bf16), V((4, 8, 32, 256), bf16), V((8, 4, 32, 256), bf16),
            V((4, 8, 32, 256), bf16), V((4, 8, 32, 256), bf16), V((8, 4, 32, 256), bf16),
            V((8, 128, 256), bf16), V((2, 128, 256), bf16), V((32, 32, 256), bf16), V((8, 32, 256), bf16),
            V((32, 256), f32),
            D((3,)), D, D((8,)), D, D((2,)), D((3,)), D((3,)), D((3,)), D((3,)), D, D, D, D, D, D,
        ],
        compiler_params=pltpu.CompilerParams(collective_id=1, has_side_effects=True,
                                             vmem_limit_bytes=56 * 1024 * 1024),
    )(near, ncnt, far, density.reshape(128, 256), positions.transpose(1, 0, 2).reshape(48, 256), areas,
      far, fcnt, left, right)
    return out.reshape(16, 8, 256)


def solution(mesh):
    grid = Mesh(mesh.devices.reshape(8, 4, 2, 4), ("z", "x", "c", "y"))
    d = ("z", "x", "c")
    return jax.shard_map(
        per_device,
        mesh=grid,
        in_specs=(
            P(d, None, None),
            P(d, None, None),
            P(d, None),
            P(d, "y", None, None, None),
            P(d, "y", None),
            P(d, "y", None, None, None),
            P(d, "y", None),
            P(d, "y", None, None, None, None),
            P(d, "y", None, None, None, None),
        ),
        out_specs=P(d, None, None),
        check_vma=False,
    )
```

time: 71.2 us -> 62.9 us (0.88)
  Pallas kernels: 69 us -> 61.2 us
    pallas_call x1, Pallas kernels: 69 us -> 61.2 us  [per_device(): pl.pallas_call(kernel, out_shape=jax.ShapeDtypeStruct((128, 256), f32), i...]
where the time goes in v3:
time: 62.9 us; the launch traced here: 62.8 us
  Pallas kernels  61.2 us (97%)
  local copies, waits for them, and re-layouts  1.57 us (2%)
    pallas_call x1, Pallas kernels, per_device(): pl.pallas_call(kernel, out_shape=jax.ShapeDtypeStruct((128, 256), f32), i...  61.2 us
    unnamed x1, local copies, waits for them, and re-layouts  1.57 us

profile of v3, /device:TPU:1, one launch (start us, length us, event | category | flops | bytes accessed | tf_op | source)
XLA Modules:
  0.0 62.8 jit_solution(16726051505490815566)
XLA Ops:
  0.0 61.2 %shard_map.91 = f32[128,256]{1,0:T(8,128)} custom-call(s32[8,64]{1,0:T(8,128)} %bitcast.26, s32[1,64]{1,0:T(1,128)} %bitcast.27, s32[4,64]{1,0:T(4,128)} %bitcast.24, bf16[128,256]{1,0:T(8,128)(2,1)} %bitcast.22, bf16[48,256]{1,0:T(8,128)(2,1)} %bitcast.23, bf16[16,256]{1,0:T(8,128)(2,1)} %area.1, s32[4,64]{1,0:T(4,128)} %bitcast.25, s32[1,64]{1,0:T(1,128)} %bitcast.28, ...), custom_call_target="tpu_custom_call" | custom-call | tf_op jit(solution)/shard_map/pallas_call | solution.py:481
  61.2 1.6 %copy.11 = f32[16,8,256]{2,1,0:T(8,128)} copy(f32[16,8,256]{2,1,0:T(8,128)} %bitcast.21) | data formatting | bytes 262144

commit v4 on v3

--- a/solution.py
+++ b/solution.py
@@ -75,7 +75,7 @@
 
 
 def kernel(near, ncnt, far, dens, pos, area, fars, fcnts, left_h, right_h, out,
-           left, right, pack, pa, pb, t1, t2, igy, igot, cvm, csm, vl, lf, rt, da, db, ub, rbuf, cbuf,
+           left, right, pack, pa, pb, t1, t2, igy, igot, cvm, csm, vl, lf, rt, da, db, ub0, ub1, rbuf, cbuf,
            acc_b, own, fc, fcy, fcr, fd, fdy, fdr, sa, sb, ra, rb, part,
            lsem, s_a, r_a, s_b, r_b, s_y, r_y, s_r, r_r, s_oa, r_oa, s_ob, r_ob, s_o, r_o):
     z, x, c, y = (lax.axis_index(n) for n in ("z", "x", "c", "y"))
@@ -232,12 +232,12 @@
         remote(igy, igot.at[row], s_r.at[0], r_r.at[0], (z, p // 2, rem(p, 2), y)).start()
 
     each(1, 8, send_i)
+    each(1, 8, lambda t: copy_a(t, row).start())
     each(4, 8, far_cols)
     step_y(lambda yy: fc.at[yy], fcy, 1)
     own_c = pltpu.make_async_copy(fc.at[y], fcy.at[y], lsem.at[1])
     own_c.start()
 
-    each(1, 8, lambda t: copy_a(t, row).start())
 
     own_i.wait()
     wait_row(igot, 0)
@@ -287,22 +287,21 @@
         return (rem(csm[2 * k, h * 32 + s], 16), h * 16 + rem(csm[2 * k + 1, h * 32 + s], 16),
                 k < csm[0, 64 + h * 32 + s])
 
-    def build(b, par, first, slot):
-        for g in range(16):
-            i, j, _ = slot_ids(b, first + g)
-            d2 = jnp.dot(rt[j], lf[par * 16 + i], preferred_element_type=f32)
-            ub[slot, g] = lax.rsqrt(d2).astype(bf16)
-
-    def apply(b, par, first, slot, rows=True, cols=True):
-        for g in range(16):
-            n = first + g
-            i, j, _ = slot_ids(b, n)
-            u = ub[slot, g]
-            if rows:
-                rbuf[8 * n:8 * n + 8, :] = jnp.dot(db[j].astype(bf16), u, preferred_element_type=f32)
-            if cols:
-                cbuf[8 * n:8 * n + 8, :] = lax.dot_general(
-                    da[par * 16 + i].astype(bf16), u, (((1,), (1,)), ((), ())), preferred_element_type=f32)
+    tiles = (ub0, ub1)
+
+    def build(b, par, n):
+        i, j, _ = slot_ids(b, n)
+        d2 = jnp.dot(rt[j], lf[par * 16 + i], preferred_element_type=f32)
+        tiles[n // 16][n % 16] = lax.rsqrt(d2).astype(bf16)
+
+    def apply(b, par, n, rows=True, cols=True):
+        i, j, _ = slot_ids(b, n)
+        u = tiles[n // 16][n % 16]
+        if rows:
+            rbuf[8 * n:8 * n + 8, :] = jnp.dot(db[j].astype(bf16), u, preferred_element_type=f32)
+        if cols:
+            cbuf[8 * n:8 * n + 8, :] = lax.dot_general(
+                da[par * 16 + i].astype(bf16), u, (((1,), (1,)), ((), ())), preferred_element_type=f32)
 
     def copy_oa(b, yy, slot):
         return remote(sa.at[b, pl.ds(pl.multiple_of(yy * 32, 32), 32)], ra.at[slot], s_oa, r_oa,
@@ -321,18 +320,21 @@
             copy_oa(b, rem(y + v, 4), me).start()
 
     acc_b[...] = jnp.zeros_like(acc_b)
-    build(row, 0, 0, 0)
+    for n in range(16):
+        build(row, 0, n)
 
     def group(t):
         b = rem(row + t, 8)
         nb = rem(row + t + 1, 8)
         par = rem(t, 2)
         copy_a(t + 1, nb).wait_recv()
-        apply(b, par, 0, 0)
-        build(b, par, 16, 1)
+        for n in range(16):
+            apply(b, par, n)
+            build(b, par, 16 + n)
         prep(lambda o: pa[nb, o:o + 16, :], 1 - par)
-        apply(b, par, 16, 1)
-        build(nb, 1 - par, 0, 0)
+        for n in range(16):
+            apply(b, par, 16 + n)
+            build(nb, 1 - par, n)
         col_sums(b)
         sums = row_sums(b)
 
@@ -367,9 +369,11 @@
         acc_b[...] += jnp.dot(pick_matrix(ids, 256), v, preferred_element_type=f32)
 
     last = rem(row + 7, 8)
-    apply(last, 1, 0, 0, rows=False)
-    build(last, 1, 16, 1)
-    apply(last, 1, 16, 1, rows=False)
+    for n in range(16):
+        apply(last, 1, n, rows=False)
+        build(last, 1, 16 + n)
+    for n in range(16):
+        apply(last, 1, 16 + n, rows=False)
     col_sums(last)
     for h in range(2):
         sb[h] = acc_b[128 * h:128 * h + 128, :].astype(bf16)
@@ -390,8 +394,8 @@
     def _():
         rb[z] = sb[half, quarter(32), :]
 
-    apply(last, 1, 0, 0, cols=False)
-    apply(last, 1, 16, 1, cols=False)
+    for n in range(32):
+        apply(last, 1, n, cols=False)
     sa[last] = row_sums(last).astype(bf16)
     send_oa(last)
 
@@ -488,7 +492,7 @@
             V((2, 192, 256), bf16), V((8, 128), i32), V((8, 128), i32), V((4, 8, 128), i32), V((8, 4, 8, 128), i32),
             V((8, 128), i32), pltpu.SMEM((8, 128), i32), V((2, 128, 128), f32), V((32, KF, 256), bf16),
             V((32, 256, KF), bf16), V((32, 8, 256), f32), V((32, 8, 256), f32),
-            V((2, 16, 256, 256), bf16), V((256, 256), f32), V((256, 256), f32), V((256, 256), f32), V((128, 256), f32),
+            V((16, 256, 256), bf16), V((16, 256, 256), bf16), V((256, 256), f32), V((256, 256), f32), V((256, 256), f32), V((128, 256), f32),
             V((4, 8, 32, 256), bf16), V((4, 8, 32, 256), bf16), V((8, 4, 32, 256), bf16),
             V((4, 8, 32, 256), bf16), V((4, 8, 32, 256), bf16), V((8, 4, 32, 256), bf16),
             V((8, 128, 256), bf16), V((2, 128, 256), bf16), V((32, 32, 256), bf16), V((8, 32, 256), bf16),

time: 62.9 us -> 58.5 us (0.930)
  Pallas kernels: 61.2 us -> 56.8 us
    pallas_call x1, Pallas kernels: 61.2 us -> 56.8 us  [per_device(): pl.pallas_call(kernel, out_shape=jax.ShapeDtypeStruct((128, 256), f32), i...]
where the time goes in v4:
time: 58.5 us; the launch traced here: 58.4 us
  Pallas kernels  56.8 us (97%)
  local copies, waits for them, and re-layouts  1.57 us (3%)
    pallas_call x1, Pallas kernels, per_device(): pl.pallas_call(kernel, out_shape=jax.ShapeDtypeStruct((128, 256), f32), i...  56.8 us
    unnamed x1, local copies, waits for them, and re-layouts  1.57 us

profile of v4, /device:TPU:1, one launch (start us, length us, event | category | flops | bytes accessed | tf_op | source)
XLA Modules:
  0.0 58.4 jit_solution(6742673626735333351)
XLA Ops:
  0.0 56.8 %shard_map.91 = f32[128,256]{1,0:T(8,128)} custom-call(s32[8,64]{1,0:T(8,128)} %bitcast.26, s32[1,64]{1,0:T(1,128)} %bitcast.27, s32[4,64]{1,0:T(4,128)} %bitcast.24, bf16[128,256]{1,0:T(8,128)(2,1)} %bitcast.22, bf16[48,256]{1,0:T(8,128)(2,1)} %bitcast.23, bf16[16,256]{1,0:T(8,128)(2,1)} %area.1, s32[4,64]{1,0:T(4,128)} %bitcast.25, s32[1,64]{1,0:T(1,128)} %bitcast.28, ...), custom_call_target="tpu_custom_call" | custom-call | tf_op jit(solution)/shard_map/pallas_call | solution.py:485
  56.8 1.6 %copy.11 = f32[16,8,256]{2,1,0:T(8,128)} copy(f32[16,8,256]{2,1,0:T(8,128)} %bitcast.21) | data formatting | bytes 262144

commit v5 on v4

--- a/solution.py
+++ b/solution.py
@@ -341,15 +341,18 @@
         @pl.when(t == 0)
         def _():
             own[...] += sums
-            wait_y(fcy, 1)
-            step_row(fcy, fcr, 1)
 
         @pl.when(t > 0)
         def _():
             sa[b] = sums.astype(bf16)
             send_oa(b)
 
-        @pl.when(t == 2)
+        @pl.when(t == 1)
+        def _():
+            wait_y(fcy, 1)
+            step_row(fcy, fcr, 1)
+
+        @pl.when(t == 3)
         def _():
             wait_y(fdy, 2)
             step_row(fdy, fdr, 2)
@@ -402,17 +405,18 @@
     wait_row(fdr, 2)
 
     def far_rows(g):
+        buf = (rbuf, cbuf)[g % 2]
         ids = []
         for b in range(4):
             p, yys = g * 2 + b // 2, (2 * (b % 2), 2 * (b % 2) + 1)
             es = [far_owner(p, yy, h) for yy in yys for h in range(2)]
-            rbuf[64 * b:64 * b + 64, :] = through(
+            buf[64 * b:64 * b + 64, :] = through(
                 jnp.concatenate([fdr[p, yy] for yy in yys], 0), jnp.concatenate([right[e] for e in es], 0),
                 jnp.concatenate([left[e] for e in es], 0), mask)
             ids += [jnp.where(k < fcnts[0, e], rem(fars[2 * k, e], 16), -1) for e in es for k in range(2)]
-        own[...] += gathered(pick_matrix(ids, 128), rbuf[...])
-
-    each(0, 4, far_rows)
+        return gathered(pick_matrix(ids, 128), buf[...])
+
+    own[...] += (far_rows(0) + far_rows(1)) + (far_rows(2) + far_rows(3))
 
     sa[row] = own[...].astype(bf16)
     for v in range(1, 4):

time: 58.5 us -> 59.6 us (1.019)
  Pallas kernels: 56.8 us -> 57.9 us
    pallas_call x1, Pallas kernels: 56.8 us -> 57.9 us  [per_device(): pl.pallas_call(kernel, out_shape=jax.ShapeDtypeStruct((128, 256), f32), i...]
where the time goes in v5:
time: 59.6 us; the launch traced here: 59.5 us
  Pallas kernels  57.9 us (97%)
  local copies, waits for them, and re-layouts  1.57 us (3%)
    pallas_call x1, Pallas kernels, per_device(): pl.pallas_call(kernel, out_shape=jax.ShapeDtypeStruct((128, 256), f32), i...  57.9 us
    unnamed x1, local copies, waits for them, and re-layouts  1.57 us

profile of v5, /device:TPU:1, one launch (start us, length us, event | category | flops | bytes accessed | tf_op | source)
XLA Modules:
  0.0 59.5 jit_solution(7127269448067419160)
XLA Ops:
  0.0 57.9 %shard_map.91 = f32[128,256]{1,0:T(8,128)} custom-call(s32[8,64]{1,0:T(8,128)} %bitcast.26, s32[1,64]{1,0:T(1,128)} %bitcast.27, s32[4,64]{1,0:T(4,128)} %bitcast.24, bf16[128,256]{1,0:T(8,128)(2,1)} %bitcast.22, bf16[48,256]{1,0:T(8,128)(2,1)} %bitcast.23, bf16[16,256]{1,0:T(8,128)(2,1)} %area.1, s32[4,64]{1,0:T(4,128)} %bitcast.25, s32[1,64]{1,0:T(1,128)} %bitcast.28, ...), custom_call_target="tpu_custom_call" | custom-call | tf_op jit(solution)/shard_map/pallas_call | solution.py:489
  57.9 1.6 %copy.11 = f32[16,8,256]{2,1,0:T(8,128)} copy(f32[16,8,256]{2,1,0:T(8,128)} %bitcast.21) | data formatting | bytes 262144

commit v6 on v4

--- a/solution.py
+++ b/solution.py
@@ -221,7 +221,11 @@
 
     cl.wait()
     cr.wait()
-    each(0, 4, far_cols)
+    def far_cols2(u):
+        far_cols(2 * u)
+        far_cols(2 * u + 1)
+
+    each(0, 2, far_cols2)
 
     wait_y(igy, 0)
     own_i = pltpu.make_async_copy(igy, igot.at[row], lsem.at[0])
@@ -233,7 +237,7 @@
 
     each(1, 8, send_i)
     each(1, 8, lambda t: copy_a(t, row).start())
-    each(4, 8, far_cols)
+    each(2, 4, far_cols2)
     step_y(lambda yy: fc.at[yy], fcy, 1)
     own_c = pltpu.make_async_copy(fc.at[y], fcy.at[y], lsem.at[1])
     own_c.start()

time: 58.5 us -> 58.3 us (level)
  no operation moved by 1% of the time
where the time goes in v6:
time: 58.3 us; the launch traced here: 58.1 us
  Pallas kernels  56.6 us (97%)
  local copies, waits for them, and re-layouts  1.57 us (3%)
    pallas_call x1, Pallas kernels, per_device(): pl.pallas_call(kernel, out_shape=jax.ShapeDtypeStruct((128, 256), f32), i...  56.6 us
    unnamed x1, local copies, waits for them, and re-layouts  1.57 us

profile of v6, /device:TPU:1, one launch (start us, length us, event | category | flops | bytes accessed | tf_op | source)
XLA Modules:
  0.0 58.1 jit_solution(1463729905435631486)
XLA Ops:
  0.0 56.6 %shard_map.91 = f32[128,256]{1,0:T(8,128)} custom-call(s32[8,64]{1,0:T(8,128)} %bitcast.26, s32[1,64]{1,0:T(1,128)} %bitcast.27, s32[4,64]{1,0:T(4,128)} %bitcast.24, bf16[128,256]{1,0:T(8,128)(2,1)} %bitcast.22, bf16[48,256]{1,0:T(8,128)(2,1)} %bitcast.23, bf16[16,256]{1,0:T(8,128)(2,1)} %area.1, s32[4,64]{1,0:T(4,128)} %bitcast.25, s32[1,64]{1,0:T(1,128)} %bitcast.28, ...), custom_call_target="tpu_custom_call" | custom-call | tf_op jit(solution)/shard_map/pallas_call | solution.py:489
  56.6 1.6 %copy.11 = f32[16,8,256]{2,1,0:T(8,128)} copy(f32[16,8,256]{2,1,0:T(8,128)} %bitcast.21) | data formatting | bytes 262144

commit v7 on v6

--- a/solution.py
+++ b/solution.py
@@ -249,7 +249,7 @@
     lists = jnp.zeros((8, 128), i32)
     for s in range(32):
         lists = jnp.where(rem(lane8, 32) == s, pltpu.roll(igot[s // 4, s % 4], rem(s - q0 + 128, 128), 1), lists)
-    cvm[...] = lists
+    cvm[...] = rem(lists, 16)
     ci = pltpu.make_async_copy(cvm, csm, lsem.at[2])
     ci.start()
     for h in range(2):
@@ -272,7 +272,7 @@
     ci.wait()
 
     def far_col(s, h, k):
-        return h * 16 + rem(csm[1 + k, 64 + h * 32 + s], 16)
+        return h * 16 + csm[1 + k, 64 + h * 32 + s]
 
     def fill_fd(p):
         for yy in range(4):
@@ -284,11 +284,12 @@
     own_d = pltpu.make_async_copy(fd.at[y], fdy.at[y], lsem.at[0])
     own_d.start()
     step_y(lambda yy: fd.at[yy], fdy, 2)
-    own_d.wait()
+    own_c2 = pltpu.make_async_copy(fcy.at[:, row], fcr.at[row], lsem.at[3])
+    own_d2 = pltpu.make_async_copy(fdy.at[:, row], fdr.at[row], lsem.at[4])
 
     def slot_ids(b, n):
         s, h, k = 4 * b + n // 8, (n // 4) % 2, n % 4
-        return (rem(csm[2 * k, h * 32 + s], 16), h * 16 + rem(csm[2 * k + 1, h * 32 + s], 16),
+        return (csm[2 * k, h * 32 + s], h * 16 + csm[2 * k + 1, h * 32 + s],
                 k < csm[0, 64 + h * 32 + s])
 
     tiles = (ub0, ub1)
@@ -347,6 +348,7 @@
             own[...] += sums
             wait_y(fcy, 1)
             step_row(fcy, fcr, 1)
+            own_c2.start()
 
         @pl.when(t > 0)
         def _():
@@ -356,16 +358,13 @@
         @pl.when(t == 2)
         def _():
             wait_y(fdy, 2)
+            own_d.wait()
             step_row(fdy, fdr, 2)
+            own_d2.start()
 
     each(0, 7, group)
 
-    own_c2 = pltpu.make_async_copy(fcy.at[:, row], fcr.at[row], lsem.at[0])
-    own_c2.start()
-    own_d2 = pltpu.make_async_copy(fdy.at[:, row], fdr.at[row], lsem.at[1])
-    own_d2.start()
     own_c2.wait()
-    own_d2.wait()
     wait_row(fcr, 1)
     for g in range(4):
         ids = [far_col(g * 8 + n // 4, (n // 2) % 2, n % 2) for n in range(32)]
@@ -403,6 +402,7 @@
     sa[last] = row_sums(last).astype(bf16)
     send_oa(last)
 
+    own_d2.wait()
     wait_row(fdr, 2)
 
     def far_rows(g):
@@ -501,7 +501,7 @@
             V((4, 8, 32, 256), bf16), V((4, 8, 32, 256), bf16), V((8, 4, 32, 256), bf16),
             V((8, 128, 256), bf16), V((2, 128, 256), bf16), V((32, 32, 256), bf16), V((8, 32, 256), bf16),
             V((32, 256), f32),
-            D((3,)), D, D((8,)), D, D((2,)), D((3,)), D((3,)), D((3,)), D((3,)), D, D, D, D, D, D,
+            D((5,)), D, D((8,)), D, D((2,)), D((3,)), D((3,)), D((3,)), D((3,)), D, D, D, D, D, D,
         ],
         compiler_params=pltpu.CompilerParams(collective_id=1, has_side_effects=True,
                                              vmem_limit_bytes=56 * 1024 * 1024),

time: 58.3 us -> 58.5 us (level)
  no operation moved by 1% of the time
where the time goes in v7:
time: 58.5 us; the launch traced here: 58.3 us
  Pallas kernels  56.8 us (97%)
  local copies, waits for them, and re-layouts  1.57 us (3%)
    pallas_call x1, Pallas kernels, per_device(): pl.pallas_call(kernel, out_shape=jax.ShapeDtypeStruct((128, 256), f32), i...  56.8 us
    unnamed x1, local copies, waits for them, and re-layouts  1.57 us

profile of v7, /device:TPU:1, one launch (start us, length us, event | category | flops | bytes accessed | tf_op | source)
XLA Modules:
  0.0 58.3 jit_solution(15253414150336857994)
XLA Ops:
  0.0 56.8 %shard_map.91 = f32[128,256]{1,0:T(8,128)} custom-call(s32[8,64]{1,0:T(8,128)} %bitcast.26, s32[1,64]{1,0:T(1,128)} %bitcast.27, s32[4,64]{1,0:T(4,128)} %bitcast.24, bf16[128,256]{1,0:T(8,128)(2,1)} %bitcast.22, bf16[48,256]{1,0:T(8,128)(2,1)} %bitcast.23, bf16[16,256]{1,0:T(8,128)(2,1)} %area.1, s32[4,64]{1,0:T(4,128)} %bitcast.25, s32[1,64]{1,0:T(1,128)} %bitcast.28, ...), custom_call_target="tpu_custom_call" | custom-call | tf_op jit(solution)/shard_map/pallas_call | solution.py:489
  56.8 1.6 %copy.11 = f32[16,8,256]{2,1,0:T(8,128)} copy(f32[16,8,256]{2,1,0:T(8,128)} %bitcast.21) | data formatting | bytes 262144

commit v8 on v7

--- a/solution.py
+++ b/solution.py
@@ -332,10 +332,10 @@
         b = rem(row + t, 8)
         nb = rem(row + t + 1, 8)
         par = rem(t, 2)
-        copy_a(t + 1, nb).wait_recv()
         for n in range(16):
             apply(b, par, n)
             build(b, par, 16 + n)
+        copy_a(t + 1, nb).wait_recv()
         prep(lambda o: pa[nb, o:o + 16, :], 1 - par)
         for n in range(16):
             apply(b, par, 16 + n)

time: 58.5 us -> 58.8 us (level)
  no operation moved by 1% of the time
where the time goes in v8:
time: 58.8 us; the launch traced here: 58.7 us
  Pallas kernels  57.1 us (97%)
  local copies, waits for them, and re-layouts  1.57 us (3%)
    pallas_call x1, Pallas kernels, per_device(): pl.pallas_call(kernel, out_shape=jax.ShapeDtypeStruct((128, 256), f32), i...  57.1 us
    unnamed x1, local copies, waits for them, and re-layouts  1.57 us

profile of v8, /device:TPU:1, one launch (start us, length us, event | category | flops | bytes accessed | tf_op | source)
XLA Modules:
  0.0 58.7 jit_solution(3851495301837643537)
XLA Ops:
  0.0 57.1 %shard_map.91 = f32[128,256]{1,0:T(8,128)} custom-call(s32[8,64]{1,0:T(8,128)} %bitcast.26, s32[1,64]{1,0:T(1,128)} %bitcast.27, s32[4,64]{1,0:T(4,128)} %bitcast.24, bf16[128,256]{1,0:T(8,128)(2,1)} %bitcast.22, bf16[48,256]{1,0:T(8,128)(2,1)} %bitcast.23, bf16[16,256]{1,0:T(8,128)(2,1)} %area.1, s32[4,64]{1,0:T(4,128)} %bitcast.25, s32[1,64]{1,0:T(1,128)} %bitcast.28, ...), custom_call_target="tpu_custom_call" | custom-call | tf_op jit(solution)/shard_map/pallas_call | solution.py:489
  57.1 1.6 %copy.11 = f32[16,8,256]{2,1,0:T(8,128)} copy(f32[16,8,256]{2,1,0:T(8,128)} %bitcast.21) | data formatting | bytes 262144
